TPU v7x, 256 devices: a whole 4x4x8 slice. The times are simulated.
256 devices in a mesh: tm: 64 (over y, x, z_lo, core), dp: 4 (over z_hi).
Axes of the slice: x: 4, y: 4, z: 8 (z_hi: 4, z_lo: 2; z = z_hi * 2 + z_lo), core: 2. Of those that a mesh axis runs over, the one named last changes fastest.
Arguments:
- resid: bfloat16 [4, 12288, 1536], P('dp', 'tm'), may hold values from -6 to 6
- qkv: bfloat16 [4, 12288, 2304], P('dp', 'tm'), may hold values from -8 to 8
- cotangent: bfloat16 [4, 12288, 1536], P('dp', 'tm'), may hold values from -16 to 16
- lengths: int32 [4], P('dp'), may hold values from 3072 to 12288, as said below
- out_proj: bfloat16 [768, 1536], replicated, may hold values from -0.21875 to 0.21875
- kernel: float32 [31, 1536], replicated, may hold values from -1 to 1
Outputs:
- d_resid: bfloat16 [4, 12288, 1536], P('dp', 'tm')
- d_qkv: bfloat16 [4, 12288, 2304], P('dp', 'tm')
- d_out_proj: float32 [768, 1536], P(None, ('tm', 'dp'))
- d_kernel: float32 [31, 1536], P(None, ('tm', 'dp'))
Inputs may be any that keep to these rules, and one draw needn't show every extreme that they name: `lengths`: valid frames come first in each utterance; one utterance has all 12288 frames valid and another a quarter of them.
All inputs are finite; a program needn't handle non-finite values.
Results may differ from a plain program's by a relative error of at most 0.029.
Values may be sent and summed in bfloat16 or wider, within the bound.
A program may use at most 128 MiB of HBM per device.

v0:
```python
import jax
import jax.numpy as jnp
from jax import lax
from jax.sharding import PartitionSpec as P

H = 8
HD = 96


NEG_FILL = -1000000000.0


def padded(block, sides, width):
    for axis, dim in sides:
        count = lax.axis_size(axis)
        forward = [(i, i + 1) for i in range(count - 1)]
        backward = [(target, source) for source, target in forward]
        low = lax.ppermute(
            lax.slice_in_dim(block, block.shape[dim] - width, None, axis=dim), axis, forward
        )
        high = lax.ppermute(lax.slice_in_dim(block, 0, width, axis=dim), axis, backward)
        block = jnp.concatenate([low, block, high], axis=dim)
    return block


def shifted(x, axis, by):
    devices = lax.axis_size(axis)
    pairs = [(i, i + by) for i in range(devices) if 0 <= i + by < devices]
    return lax.ppermute(x, axis, pairs)


def head_scores(q_head, k_head, key_open):
    scores = lax.dot_general(
        q_head, k_head, (((1,), (1,)), ((), ())), preferred_element_type=jnp.float32
    )
    return jnp.where(key_open[None, :], scores * HD ** (-0.5), NEG_FILL)


def silu_slope(values):
    sigma = jax.nn.sigmoid(values)
    return sigma * (1.0 + values * (1.0 - sigma))


def attend(queries, key_values, key_open, query_valid):
    attn_width = queries.shape[1]
    results = []
    totals = []
    for head_index in range(H):
        first_col = head_index * HD
        last_col = first_col + HD
        scores = head_scores(
            queries[:, first_col:last_col], key_values[:, first_col:last_col], key_open
        )
        row_peak = jnp.max(scores, axis=1, keepdims=True)
        summed = jnp.sum(jnp.exp(scores - row_peak), axis=1, keepdims=True)
        log_total = row_peak + jnp.log(summed)
        weights = jnp.exp(scores - log_total).astype(jnp.bfloat16)
        values_head = key_values[:, attn_width + first_col : attn_width + last_col]
        results.append(jnp.dot(weights, values_head, preferred_element_type=jnp.float32))
        totals.append(log_total)
    attended = (jnp.concatenate(results, axis=1) * query_valid[:, None]).astype(jnp.bfloat16)
    return (attended, jnp.concatenate(totals, axis=1))


def grad_heads(queries, key_values, key_open, attended_grad, log_totals, deltas):
    attn_width = queries.shape[1]
    query_cols = []
    key_cols = []
    value_cols = []
    for head_index in range(H):
        first_col = head_index * HD
        last_col = first_col + HD
        q_head = queries[:, first_col:last_col]
        k_head = key_values[:, first_col:last_col]
        v_head = key_values[:, attn_width + first_col : attn_width + last_col]
        grad_head = attended_grad[:, first_col:last_col]
        scores = head_scores(q_head, k_head, key_open)
        weights = jnp.exp(scores - log_totals[:, head_index : head_index + 1])
        slopes = lax.dot_general(
            grad_head, v_head, (((1,), (1,)), ((), ())), preferred_element_type=jnp.float32
        )
        dscore = (
            weights * (slopes - deltas[:, head_index : head_index + 1]) * HD ** (-0.5)
        ).astype(jnp.bfloat16)
        query_cols.append(jnp.dot(dscore, k_head, preferred_element_type=jnp.float32))
        key_cols.append(
            lax.dot_general(
                dscore, q_head, (((0,), (0,)), ((), ())), preferred_element_type=jnp.float32
            )
        )
        value_cols.append(
            lax.dot_general(
                weights.astype(jnp.bfloat16),
                grad_head,
                (((0,), (0,)), ((), ())),
                preferred_element_type=jnp.float32,
            )
        )
    query_grad = jnp.concatenate(query_cols, axis=1)
    pair_grad = jnp.concatenate(key_cols + value_cols, axis=1)
    return (query_grad, pair_grad)


def local(resid, qkv, cotangent, lengths, out_proj, kernel):
    shard_rows = resid.shape[1]
    model_width = resid.shape[2]
    attn_width = out_proj.shape[0]
    taps = kernel.shape[0]
    reach = (taps - 1) // 2
    utter_length = lengths[0]
    first_frame = lax.axis_index("tm") * shard_rows
    frame_index = first_frame + jnp.arange(shard_rows, dtype=jnp.int32)
    own_open = frame_index < utter_length
    query_valid = own_open.astype(jnp.float32)
    key_index = first_frame - shard_rows + jnp.arange(3 * shard_rows, dtype=jnp.int32)
    key_open = (key_index >= 0) & (key_index < utter_length)
    queries = qkv[0, :, :attn_width]
    pairs = qkv[0, :, attn_width:]
    near_pairs = padded(pairs, (("tm", 0),), shard_rows)
    attended, log_totals = attend(queries, near_pairs, key_open, query_valid)
    mixed_in = (
        resid[0].astype(jnp.float32)
        + jnp.dot(attended, out_proj, preferred_element_type=jnp.float32)
    ).astype(jnp.bfloat16)
    masked = (mixed_in.astype(jnp.float32) * query_valid[:, None]).astype(jnp.bfloat16)
    masked_rim = padded(masked, (("tm", 0),), reach)
    conv_out = jnp.zeros((shard_rows, model_width), jnp.float32)
    for tap_index in range(taps):
        conv_out = conv_out + kernel[tap_index] * masked_rim[
            tap_index : tap_index + shard_rows
        ].astype(jnp.float32)
    cot_here = cotangent[0].astype(jnp.float32)
    conv_grad = (cot_here * silu_slope(conv_out)).astype(jnp.bfloat16)
    grad_rim = padded(conv_grad, (("tm", 0),), reach)
    conv_grad_wide = conv_grad.astype(jnp.float32)
    back_conv = jnp.zeros((shard_rows, model_width), jnp.float32)
    kernel_rows = []
    for tap_index in range(taps):
        back_conv = back_conv + kernel[tap_index] * grad_rim[
            2 * reach - tap_index : 2 * reach - tap_index + shard_rows
        ].astype(jnp.float32)
        kernel_rows.append(
            jnp.sum(
                conv_grad_wide * masked_rim[tap_index : tap_index + shard_rows].astype(jnp.float32),
                axis=0,
            )
        )
    kernel_term = jnp.stack(kernel_rows, axis=0)
    resid_grad = (cot_here + query_valid[:, None] * back_conv).astype(jnp.bfloat16)
    proj_term = lax.dot_general(
        attended, resid_grad, (((0,), (0,)), ((), ())), preferred_element_type=jnp.float32
    )
    proj_grad, kernel_grad = (
        lax.psum_scatter(proj_term, ("tm", "dp"), scatter_dimension=1, tiled=True),
        lax.psum_scatter(kernel_term, ("tm", "dp"), scatter_dimension=1, tiled=True),
    )
    attended_grad = (
        query_valid[:, None]
        * lax.dot_general(
            resid_grad, out_proj, (((1,), (1,)), ((), ())), preferred_element_type=jnp.float32
        )
    ).astype(jnp.bfloat16)
    deltas = jnp.sum(
        (attended_grad.astype(jnp.float32) * attended.astype(jnp.float32)).reshape(
            shard_rows, H, HD
        ),
        axis=2,
    )
    query_grad, pair_parts = grad_heads(
        queries, near_pairs, key_open, attended_grad, log_totals, deltas
    )
    from_before = shifted(pair_parts[2 * shard_rows :].astype(jnp.bfloat16), "tm", 1).astype(
        jnp.float32
    )
    from_after = shifted(pair_parts[:shard_rows].astype(jnp.bfloat16), "tm", -1).astype(jnp.float32)
    pair_grad = pair_parts[shard_rows : 2 * shard_rows] + from_before + from_after
    qkv_grad = jnp.concatenate(
        [query_grad.astype(jnp.bfloat16), pair_grad.astype(jnp.bfloat16)], axis=1
    )
    return (resid_grad[None], qkv_grad[None], proj_grad, kernel_grad)


def solution(mesh):
    in_specs = (P("dp", "tm", None), P("dp", "tm", None), P("dp", "tm", None), P("dp"), P(), P())
    out_specs = (
        P("dp", "tm", None),
        P("dp", "tm", None),
        P(None, ("tm", "dp")),
        P(None, ("tm", "dp")),
    )
    return jax.shard_map(local, mesh=mesh, in_specs=in_specs, out_specs=out_specs, check_vma=False)
```

profile of v0, /device:TPU:1, one launch (start us, length us, event | category | flops | bytes accessed | tf_op | source)
XLA Modules:
  0.0 1420.5 jit_solution(8514459791389625408)
XLA Ops:
  8.5 5.1 collective-permute-start.1
  16.8 2.4 slice_reduce_fusion.38
  20.2 3.3 collective-permute-done.1
  36.0 1.9 fusion.4
  38.6 3.3 collective-permute-start.2
  43.9 2.1 slice_reduce_fusion.37
  46.0 2.9 collective-permute-done.3
  49.5 10.5 fusion.116
  62.6 3.8 collective-permute-start.5
  71.2 2.8 stack.127
  74.0 8.7 fusion.69
  93.4 3.0 fusion.278
  96.4 691.2 %fusion = f32[768,8]{0,1:T(8,128)S(1)} fusion(f32[768,1536]{0,1:T(8,128)} %fusion.278), kind=kCustom, calls=%all-reduce-scatter | all-reduce-scatter fusion | flops 1572865 | bytes 4743168
  792.2 8.6 collective-permute-start.67
  805.4 2.0 fusion.239
  812.6 7.8 collective-permute-start.71
  838.2 13.5 collective-permute-start.55
  851.7 8.2 collective-permute-start.54
  861.0 4.8 collective-permute-start.53
  865.7 3.0 collective-permute-start.52
  872.5 2.4 collective-permute-start.49
  875.9 5.2 concatenate.91
  881.1 2.2 convert.38
  887.1 2.4 collective-permute-start.46
  889.5 2.4 collective-permute-start.45
  892.0 3.8 collective-permute-start.44
  896.9 2.3 collective-permute-start.43
  899.2 3.7 collective-permute-start.42
  903.0 2.8 collective-permute-start.41
  908.8 3.1 collective-permute-start.38
  912.0 4.4 collective-permute-start.37
  916.3 13.1 collective-permute-start.36
  929.5 13.1 collective-permute-start.35
  942.7 13.1 collective-permute-start.34
  956.0 13.1 collective-permute-start.33
  969.2 13.1 collective-permute-start.32
  982.3 13.1 collective-permute-start.31
  995.5 13.1 collective-permute-start.30
  1008.7 13.1 collective-permute-start.29
  1022.2 13.2 collective-permute-start.28
  1035.5 13.1 collective-permute-start.27
  1048.6 13.1 collective-permute-start.26
  1061.8 13.1 collective-permute-start.25
  1074.9 13.1 collective-permute-start.24
  1089.0 13.1 collective-permute-start.23
  1102.1 13.1 collective-permute-start.22
  1115.3 13.1 collective-permute-start.21
  1128.4 13.1 collective-permute-start.20
  1141.6 13.1 collective-permute-start.19
  1155.6 13.1 collective-permute-start.18
  1168.8 13.1 collective-permute-start.17
  1181.9 13.1 collective-permute-start.16
  1195.1 13.1 collective-permute-start.15
  1208.2 13.1 collective-permute-start.14
  1222.2 13.1 collective-permute-start.13
  1235.3 13.1 collective-permute-start.12
  1248.5 13.1 collective-permute-start.11
  1261.6 3.7 collective-permute-start.6
  1265.3 2.4 collective-permute-start.7
  1268.6 13.6 collective-permute-start.10
  1282.2 13.1 collective-permute-start.9
  1295.4 13.1 collective-permute-start.8
  1309.1 6.4 collective-permute-done.8
  1315.5 92.2 %concatenate.93 = f32[768,518]{0,1:T(8,128)} concatenate(f32[768,6]{0,1:T(8,128)S(1)} %collective-permute-done.71, f32[768,8]{0,1:T(8,128)S(1)} %collective-permute-done.70, f32[768,8]{0,1:T(8,128)S(1)} %copy-done.58, f32[768,8]{0,1:T(8,128)S(1)} %copy-done.60, f32[768,8]{0,1:T(8,128)} %collective-permute-done.67, f32[768,8]{0,1:T(8,128)S(1)} %collective-permute-done.66, ...), dimensions={1} | concatenate | bytes 3182592
  (467 shorter events, 93.8 us)
Async XLA Ops:
  7.2 1401.9 %all-reduce.5.cloned.1.call-start = ((), (), s32[]{:S(2)}) async-start(), calls=%async_computation | async-start | bytes 393216
  8.5 15.1 %collective-permute-start.1 = (bf16[192,1536]{1,0:T(8,128)(2,1)S(1)}, bf16[192,1536]{1,0:T(8,128)(2,1)S(1)}, u32[]{:S(2)}, u32[]{:S(2)}) collective-permute-start(bf16[192,1536]{1,0:T(8,128)(2,1)S(1)} %slice_bitcast_fusion), channel_id=1, source_target_pairs={{4,0},{8,4},{12,8},{16,12},{20,16},{24,20},{28,24},{32,28},{36,32}... | collective-permute-start | bytes 1769480 | tf_op jit(solution)/shard_map/ppermute | solution.py:21
  13.6 9.9 collective-permute-start
  60.7 13.3 collective-permute-start.4
  62.6 11.4 collective-permute-start.5
  788.3 34.6 %collective-permute-start.70 = (f32[768,8]{0,1:T(8,128)S(1)}, f32[768,8]{0,1:T(8,128)S(1)}, u32[]{:S(2)}, u32[]{:S(2)}) collective-permute-start(f32[768,8]{0,1:T(8,128)S(1)} %fusion), channel_id=1, source_target_pairs={{0,63},{1,64},{2,65},{3,66},{4,67},{5,68},{6,69},{7,70},{8,71},{9,... | collective-permute-start | bytes 73736
  789.6 34.6 %collective-permute-start.69 = (f32[768,8]{0,1:T(8,128)S(1)}, f32[768,8]{0,1:T(8,128)S(1)}, u32[]{:S(2)}, u32[]{:S(2)}) collective-permute-start(f32[768,8]{0,1:T(8,128)S(1)} %fusion), channel_id=1, source_target_pairs={{0,62},{1,63},{2,64},{3,65},{4,66},{5,67},{6,68},{7,69},{8,70},{9,... | collective-permute-start | bytes 73736
  790.9 35.9 %collective-permute-start.68 = (f32[768,8]{0,1:T(8,128)S(1)}, f32[768,8]{0,1:T(8,128)S(1)}, u32[]{:S(2)}, u32[]{:S(2)}) collective-permute-start(f32[768,8]{0,1:T(8,128)S(1)} %fusion), channel_id=1, source_target_pairs={{0,61},{1,62},{2,63},{3,64},{4,65},{5,66},{6,67},{7,68},{8,69},{9,... | collective-permute-start | bytes 73736
  792.2 35.9 %collective-permute-start.67 = (f32[768,8]{0,1:T(8,128)S(1)}, f32[768,8]{0,1:T(8,128)}, u32[]{:S(2)}, u32[]{:S(2)}) collective-permute-start(f32[768,8]{0,1:T(8,128)S(1)} %fusion), channel_id=1, source_target_pairs={{0,60},{1,61},{2,62},{3,63},{4,64},{5,65},{6,66},{7,67},{8,68},{9,... | collective-permute-start | bytes 73736
  812.6 8.8 collective-permute-start.71
  832.0 19.7 %collective-permute-start.59 = (f32[768,8]{0,1:T(8,128)S(1)}, f32[768,8]{0,1:T(8,128)S(1)}, u32[]{:S(2)}, u32[]{:S(2)}) collective-permute-start(f32[768,8]{0,1:T(8,128)S(1)} %fusion), channel_id=1, source_target_pairs={{0,52},{1,53},{2,54},{3,55},{4,56},{5,57},{6,58},{7,59},{8,60},{9,... | collective-permute-start | bytes 73736
  834.3 26.6 %collective-permute-start.58 = (f32[768,8]{0,1:T(8,128)S(1)}, f32[768,8]{0,1:T(8,128)S(1)}, u32[]{:S(2)}, u32[]{:S(2)}) collective-permute-start(f32[768,8]{0,1:T(8,128)S(1)} %fusion), channel_id=1, source_target_pairs={{0,51},{1,52},{2,53},{3,54},{4,55},{5,56},{6,57},{7,58},{8,59},{9,... | collective-permute-start | bytes 73736
  835.6 30.1 %collective-permute-start.57 = (f32[768,8]{0,1:T(8,128)S(1)}, f32[768,8]{0,1:T(8,128)S(1)}, u32[]{:S(2)}, u32[]{:S(2)}) collective-permute-start(f32[768,8]{0,1:T(8,128)S(1)} %fusion), channel_id=1, source_target_pairs={{0,50},{1,51},{2,52},{3,53},{4,54},{5,55},{6,56},{7,57},{8,58},{9,... | collective-permute-start | bytes 73736
  836.9 31.8 %collective-permute-start.56 = (f32[768,8]{0,1:T(8,128)S(1)}, f32[768,8]{0,1:T(8,128)S(1)}, u32[]{:S(2)}, u32[]{:S(2)}) collective-permute-start(f32[768,8]{0,1:T(8,128)S(1)} %fusion), channel_id=1, source_target_pairs={{0,49},{1,50},{2,51},{3,52},{4,53},{5,54},{6,55},{7,56},{8,57},{9,... | collective-permute-start | bytes 73736
  838.2 32.4 %collective-permute-start.55 = (f32[768,8]{0,1:T(8,128)S(1)}, f32[768,8]{0,1:T(8,128)S(1)}, u32[]{:S(2)}, u32[]{:S(2)}) collective-permute-start(f32[768,8]{0,1:T(8,128)S(1)} %fusion), channel_id=1, source_target_pairs={{0,48},{1,49},{2,50},{3,51},{4,52},{5,53},{6,54},{7,55},{8,56},{9,... | collective-permute-start | bytes 73736
  851.7 20.7 %collective-permute-start.54 = (f32[768,8]{0,1:T(8,128)S(1)}, f32[768,8]{0,1:T(8,128)S(1)}, u32[]{:S(2)}, u32[]{:S(2)}) collective-permute-start(f32[768,8]{0,1:T(8,128)S(1)} %fusion), channel_id=1, source_target_pairs={{0,47},{1,48},{2,49},{3,50},{4,51},{5,52},{6,53},{7,54},{8,55},{9,... | collective-permute-start | bytes 73736
  861.0 22.4 %collective-permute-start.53 = (f32[768,8]{0,1:T(8,128)S(1)}, f32[768,8]{0,1:T(8,128)}, u32[]{:S(2)}, u32[]{:S(2)}) collective-permute-start(f32[768,8]{0,1:T(8,128)S(1)} %fusion), channel_id=1, source_target_pairs={{0,46},{1,47},{2,48},{3,49},{4,50},{5,51},{6,52},{7,53},{8,54},{9,... | collective-permute-start | bytes 73736
  865.7 19.5 %collective-permute-start.52 = (f32[768,8]{0,1:T(8,128)S(1)}, f32[768,8]{0,1:T(8,128)}, u32[]{:S(2)}, u32[]{:S(2)}) collective-permute-start(f32[768,8]{0,1:T(8,128)S(1)} %fusion), channel_id=1, source_target_pairs={{0,45},{1,46},{2,47},{3,48},{4,49},{5,50},{6,51},{7,52},{8,53},{9,... | collective-permute-start | bytes 73736
  868.7 18.4 %collective-permute-start.51 = (f32[768,8]{0,1:T(8,128)S(1)}, f32[768,8]{0,1:T(8,128)}, u32[]{:S(2)}, u32[]{:S(2)}) collective-permute-start(f32[768,8]{0,1:T(8,128)S(1)} %fusion), channel_id=1, source_target_pairs={{0,44},{1,45},{2,46},{3,47},{4,48},{5,49},{6,50},{7,51},{8,52},{9,... | collective-permute-start | bytes 73736
  870.6 18.9 %collective-permute-start.50 = (f32[768,8]{0,1:T(8,128)S(1)}, f32[768,8]{0,1:T(8,128)}, u32[]{:S(2)}, u32[]{:S(2)}) collective-permute-start(f32[768,8]{0,1:T(8,128)S(1)} %fusion), channel_id=1, source_target_pairs={{0,43},{1,44},{2,45},{3,46},{4,47},{5,48},{6,49},{7,50},{8,51},{9,... | collective-permute-start | bytes 73736
  872.5 19.5 %collective-permute-start.49 = (f32[768,8]{0,1:T(8,128)S(1)}, f32[768,8]{0,1:T(8,128)}, u32[]{:S(2)}, u32[]{:S(2)}) collective-permute-start(f32[768,8]{0,1:T(8,128)S(1)} %fusion), channel_id=1, source_target_pairs={{0,42},{1,43},{2,44},{3,45},{4,46},{5,47},{6,48},{7,49},{8,50},{9,... | collective-permute-start | bytes 73736
  883.4 13.5 collective-permute-start.48
  885.3 14.0 collective-permute-start.47
  887.1 15.9 %collective-permute-start.46 = (f32[768,8]{0,1:T(8,128)S(1)}, f32[768,8]{0,1:T(8,128)S(1)}, u32[]{:S(2)}, u32[]{:S(2)}) collective-permute-start(f32[768,8]{0,1:T(8,128)S(1)} %fusion), channel_id=1, source_target_pairs={{0,39},{1,40},{2,41},{3,42},{4,43},{5,44},{6,45},{7,46},{8,47},{9,... | collective-permute-start | bytes 73736
  889.5 16.3 %collective-permute-start.45 = (f32[768,8]{0,1:T(8,128)S(1)}, f32[768,8]{0,1:T(8,128)S(1)}, u32[]{:S(2)}, u32[]{:S(2)}) collective-permute-start(f32[768,8]{0,1:T(8,128)S(1)} %fusion), channel_id=1, source_target_pairs={{0,38},{1,39},{2,40},{3,41},{4,42},{5,43},{6,44},{7,45},{8,46},{9,... | collective-permute-start | bytes 73736
  892.0 15.2 %collective-permute-start.44 = (f32[768,8]{0,1:T(8,128)S(1)}, f32[768,8]{0,1:T(8,128)S(1)}, u32[]{:S(2)}, u32[]{:S(2)}) collective-permute-start(f32[768,8]{0,1:T(8,128)S(1)} %fusion), channel_id=1, source_target_pairs={{0,37},{1,38},{2,39},{3,40},{4,41},{5,42},{6,43},{7,44},{8,45},{9,... | collective-permute-start | bytes 73736
  896.9 11.9 collective-permute-start.43
  899.2 12.7 collective-permute-start.42
  903.0 13.3 collective-permute-start.41
  905.8 23.6 %collective-permute-start.40 = (f32[768,8]{0,1:T(8,128)S(1)}, f32[768,8]{0,1:T(8,128)S(1)}, u32[]{:S(2)}, u32[]{:S(2)}) collective-permute-start(f32[768,8]{0,1:T(8,128)S(1)} %fusion), channel_id=1, source_target_pairs={{0,33},{1,34},{2,35},{3,36},{4,37},{5,38},{6,39},{7,40},{8,41},{9,... | collective-permute-start | bytes 73736
  907.2 35.5 %collective-permute-start.39 = (f32[768,8]{0,1:T(8,128)S(1)}, f32[768,8]{0,1:T(8,128)S(1)}, u32[]{:S(2)}, u32[]{:S(2)}) collective-permute-start(f32[768,8]{0,1:T(8,128)S(1)} %fusion), channel_id=1, source_target_pairs={{0,32},{1,33},{2,34},{3,35},{4,36},{5,37},{6,38},{7,39},{8,40},{9,... | collective-permute-start | bytes 73736
  908.8 47.2 %collective-permute-start.38 = (f32[768,8]{0,1:T(8,128)S(1)}, f32[768,8]{0,1:T(8,128)S(1)}, u32[]{:S(2)}, u32[]{:S(2)}) collective-permute-start(f32[768,8]{0,1:T(8,128)S(1)} %fusion), channel_id=1, source_target_pairs={{0,31},{1,32},{2,33},{3,34},{4,35},{5,36},{6,37},{7,38},{8,39},{9,... | collective-permute-start | bytes 73736
  912.0 57.2 %collective-permute-start.37 = (f32[768,8]{0,1:T(8,128)S(1)}, f32[768,8]{0,1:T(8,128)S(1)}, u32[]{:S(2)}, u32[]{:S(2)}) collective-permute-start(f32[768,8]{0,1:T(8,128)S(1)} %fusion), channel_id=1, source_target_pairs={{0,30},{1,31},{2,32},{3,33},{4,34},{5,35},{6,36},{7,37},{8,38},{9,... | collective-permute-start | bytes 73736
  916.3 66.0 %collective-permute-start.36 = (f32[768,8]{0,1:T(8,128)S(1)}, f32[768,8]{0,1:T(8,128)S(1)}, u32[]{:S(2)}, u32[]{:S(2)}) collective-permute-start(f32[768,8]{0,1:T(8,128)S(1)} %fusion), channel_id=1, source_target_pairs={{0,29},{1,30},{2,31},{3,32},{4,33},{5,34},{6,35},{7,36},{8,37},{9,... | collective-permute-start | bytes 73736
  929.5 66.0 %collective-permute-start.35 = (f32[768,8]{0,1:T(8,128)S(1)}, f32[768,8]{0,1:T(8,128)S(1)}, u32[]{:S(2)}, u32[]{:S(2)}) collective-permute-start(f32[768,8]{0,1:T(8,128)S(1)} %fusion), channel_id=1, source_target_pairs={{0,28},{1,29},{2,30},{3,31},{4,32},{5,33},{6,34},{7,35},{8,36},{9,... | collective-permute-start | bytes 73736
  942.7 66.0 %collective-permute-start.34 = (f32[768,8]{0,1:T(8,128)S(1)}, f32[768,8]{0,1:T(8,128)S(1)}, u32[]{:S(2)}, u32[]{:S(2)}) collective-permute-start(f32[768,8]{0,1:T(8,128)S(1)} %fusion), channel_id=1, source_target_pairs={{0,27},{1,28},{2,29},{3,30},{4,31},{5,32},{6,33},{7,34},{8,35},{9,... | collective-permute-start | bytes 73736
  956.0 66.1 %collective-permute-start.33 = (f32[768,8]{0,1:T(8,128)S(1)}, f32[768,8]{0,1:T(8,128)S(1)}, u32[]{:S(2)}, u32[]{:S(2)}) collective-permute-start(f32[768,8]{0,1:T(8,128)S(1)} %fusion), channel_id=1, source_target_pairs={{0,26},{1,27},{2,28},{3,29},{4,30},{5,31},{6,32},{7,33},{8,34},{9,... | collective-permute-start | bytes 73736
  969.2 66.3 %collective-permute-start.32 = (f32[768,8]{0,1:T(8,128)S(1)}, f32[768,8]{0,1:T(8,128)S(1)}, u32[]{:S(2)}, u32[]{:S(2)}) collective-permute-start(f32[768,8]{0,1:T(8,128)S(1)} %fusion), channel_id=1, source_target_pairs={{0,25},{1,26},{2,27},{3,28},{4,29},{5,30},{6,31},{7,32},{8,33},{9,... | collective-permute-start | bytes 73736
  982.3 66.3 %collective-permute-start.31 = (f32[768,8]{0,1:T(8,128)S(1)}, f32[768,8]{0,1:T(8,128)S(1)}, u32[]{:S(2)}, u32[]{:S(2)}) collective-permute-start(f32[768,8]{0,1:T(8,128)S(1)} %fusion), channel_id=1, source_target_pairs={{0,24},{1,25},{2,26},{3,27},{4,28},{5,29},{6,30},{7,31},{8,32},{9,... | collective-permute-start | bytes 73736
  995.5 66.3 %collective-permute-start.30 = (f32[768,8]{0,1:T(8,128)S(1)}, f32[768,8]{0,1:T(8,128)S(1)}, u32[]{:S(2)}, u32[]{:S(2)}) collective-permute-start(f32[768,8]{0,1:T(8,128)S(1)} %fusion), channel_id=1, source_target_pairs={{0,23},{1,24},{2,25},{3,26},{4,27},{5,28},{6,29},{7,30},{8,31},{9,... | collective-permute-start | bytes 73736
  1008.7 66.3 %collective-permute-start.29 = (f32[768,8]{0,1:T(8,128)S(1)}, f32[768,8]{0,1:T(8,128)S(1)}, u32[]{:S(2)}, u32[]{:S(2)}) collective-permute-start(f32[768,8]{0,1:T(8,128)S(1)} %fusion), channel_id=1, source_target_pairs={{0,22},{1,23},{2,24},{3,25},{4,26},{5,27},{6,28},{7,29},{8,30},{9,... | collective-permute-start | bytes 73736
  1022.2 66.8 %collective-permute-start.28 = (f32[768,8]{0,1:T(8,128)S(1)}, f32[768,8]{0,1:T(8,128)S(1)}, u32[]{:S(2)}, u32[]{:S(2)}) collective-permute-start(f32[768,8]{0,1:T(8,128)S(1)} %fusion), channel_id=1, source_target_pairs={{0,21},{1,22},{2,23},{3,24},{4,25},{5,26},{6,27},{7,28},{8,29},{9,... | collective-permute-start | bytes 73736
  1035.5 66.6 %collective-permute-start.27 = (f32[768,8]{0,1:T(8,128)S(1)}, f32[768,8]{0,1:T(8,128)S(1)}, u32[]{:S(2)}, u32[]{:S(2)}) collective-permute-start(f32[768,8]{0,1:T(8,128)S(1)} %fusion), channel_id=1, source_target_pairs={{0,20},{1,21},{2,22},{3,23},{4,24},{5,25},{6,26},{7,27},{8,28},{9,... | collective-permute-start | bytes 73736
  1048.6 66.6 %collective-permute-start.26 = (f32[768,8]{0,1:T(8,128)S(1)}, f32[768,8]{0,1:T(8,128)S(1)}, u32[]{:S(2)}, u32[]{:S(2)}) collective-permute-start(f32[768,8]{0,1:T(8,128)S(1)} %fusion), channel_id=1, source_target_pairs={{0,19},{1,20},{2,21},{3,22},{4,23},{5,24},{6,25},{7,26},{8,27},{9,... | collective-permute-start | bytes 73736
  1061.8 66.6 %collective-permute-start.25 = (f32[768,8]{0,1:T(8,128)S(1)}, f32[768,8]{0,1:T(8,128)S(1)}, u32[]{:S(2)}, u32[]{:S(2)}) collective-permute-start(f32[768,8]{0,1:T(8,128)S(1)} %fusion), channel_id=1, source_target_pairs={{0,18},{1,19},{2,20},{3,21},{4,22},{5,23},{6,24},{7,25},{8,26},{9,... | collective-permute-start | bytes 73736
  1074.9 66.6 %collective-permute-start.24 = (f32[768,8]{0,1:T(8,128)S(1)}, f32[768,8]{0,1:T(8,128)S(1)}, u32[]{:S(2)}, u32[]{:S(2)}) collective-permute-start(f32[768,8]{0,1:T(8,128)S(1)} %fusion), channel_id=1, source_target_pairs={{0,17},{1,18},{2,19},{3,20},{4,21},{5,22},{6,23},{7,24},{8,25},{9,... | collective-permute-start | bytes 73736
  1089.0 66.7 %collective-permute-start.23 = (f32[768,8]{0,1:T(8,128)S(1)}, f32[768,8]{0,1:T(8,128)S(1)}, u32[]{:S(2)}, u32[]{:S(2)}) collective-permute-start(f32[768,8]{0,1:T(8,128)S(1)} %fusion), channel_id=1, source_target_pairs={{0,16},{1,17},{2,18},{3,19},{4,20},{5,21},{6,22},{7,23},{8,24},{9,... | collective-permute-start | bytes 73736
  1102.1 66.6 %collective-permute-start.22 = (f32[768,8]{0,1:T(8,128)S(1)}, f32[768,8]{0,1:T(8,128)S(1)}, u32[]{:S(2)}, u32[]{:S(2)}) collective-permute-start(f32[768,8]{0,1:T(8,128)S(1)} %fusion), channel_id=1, source_target_pairs={{0,15},{1,16},{2,17},{3,18},{4,19},{5,20},{6,21},{7,22},{8,23},{9,... | collective-permute-start | bytes 73736
  1115.3 66.6 %collective-permute-start.21 = (f32[768,8]{0,1:T(8,128)S(1)}, f32[768,8]{0,1:T(8,128)S(1)}, u32[]{:S(2)}, u32[]{:S(2)}) collective-permute-start(f32[768,8]{0,1:T(8,128)S(1)} %fusion), channel_id=1, source_target_pairs={{0,14},{1,15},{2,16},{3,17},{4,18},{5,19},{6,20},{7,21},{8,22},{9,... | collective-permute-start | bytes 73736
  1128.4 66.6 %collective-permute-start.20 = (f32[768,8]{0,1:T(8,128)S(1)}, f32[768,8]{0,1:T(8,128)S(1)}, u32[]{:S(2)}, u32[]{:S(2)}) collective-permute-start(f32[768,8]{0,1:T(8,128)S(1)} %fusion), channel_id=1, source_target_pairs={{0,13},{1,14},{2,15},{3,16},{4,17},{5,18},{6,19},{7,20},{8,21},{9,... | collective-permute-start | bytes 73736
  1141.6 66.6 %collective-permute-start.19 = (f32[768,8]{0,1:T(8,128)S(1)}, f32[768,8]{0,1:T(8,128)S(1)}, u32[]{:S(2)}, u32[]{:S(2)}) collective-permute-start(f32[768,8]{0,1:T(8,128)S(1)} %fusion), channel_id=1, source_target_pairs={{0,12},{1,13},{2,14},{3,15},{4,16},{5,17},{6,18},{7,19},{8,20},{9,... | collective-permute-start | bytes 73736
  1155.6 66.6 %collective-permute-start.18 = (f32[768,8]{0,1:T(8,128)S(1)}, f32[768,8]{0,1:T(8,128)S(1)}, u32[]{:S(2)}, u32[]{:S(2)}) collective-permute-start(f32[768,8]{0,1:T(8,128)S(1)} %fusion), channel_id=1, source_target_pairs={{0,11},{1,12},{2,13},{3,14},{4,15},{5,16},{6,17},{7,18},{8,19},{9,... | collective-permute-start | bytes 73736
  1168.8 66.5 %collective-permute-start.17 = (f32[768,8]{0,1:T(8,128)S(1)}, f32[768,8]{0,1:T(8,128)S(1)}, u32[]{:S(2)}, u32[]{:S(2)}) collective-permute-start(f32[768,8]{0,1:T(8,128)S(1)} %fusion), channel_id=1, source_target_pairs={{0,10},{1,11},{2,12},{3,13},{4,14},{5,15},{6,16},{7,17},{8,18},{9,... | collective-permute-start | bytes 73736
  1181.9 66.5 %collective-permute-start.16 = (f32[768,8]{0,1:T(8,128)S(1)}, f32[768,8]{0,1:T(8,128)S(1)}, u32[]{:S(2)}, u32[]{:S(2)}) collective-permute-start(f32[768,8]{0,1:T(8,128)S(1)} %fusion), channel_id=1, source_target_pairs={{0,9},{1,10},{2,11},{3,12},{4,13},{5,14},{6,15},{7,16},{8,17},{9,1... | collective-permute-start | bytes 73736
  1195.1 66.6 %collective-permute-start.15 = (f32[768,8]{0,1:T(8,128)S(1)}, f32[768,8]{0,1:T(8,128)S(1)}, u32[]{:S(2)}, u32[]{:S(2)}) collective-permute-start(f32[768,8]{0,1:T(8,128)S(1)} %fusion), channel_id=1, source_target_pairs={{0,8},{1,9},{2,10},{3,11},{4,12},{5,13},{6,14},{7,15},{8,16},{9,17... | collective-permute-start | bytes 73736
  1208.2 57.1 %collective-permute-start.14 = (f32[768,8]{0,1:T(8,128)S(1)}, f32[768,8]{0,1:T(8,128)S(1)}, u32[]{:S(2)}, u32[]{:S(2)}) collective-permute-start(f32[768,8]{0,1:T(8,128)S(1)} %fusion), channel_id=1, source_target_pairs={{0,7},{1,8},{2,9},{3,10},{4,11},{5,12},{6,13},{7,14},{8,15},{9,16}... | collective-permute-start | bytes 73736
  1222.2 46.4 %collective-permute-start.13 = (f32[768,8]{0,1:T(8,128)S(1)}, f32[768,8]{0,1:T(8,128)S(1)}, u32[]{:S(2)}, u32[]{:S(2)}) collective-permute-start(f32[768,8]{0,1:T(8,128)S(1)} %fusion), channel_id=1, source_target_pairs={{0,6},{1,7},{2,8},{3,9},{4,10},{5,11},{6,12},{7,13},{8,14},{9,15},... | collective-permute-start | bytes 73736
  1235.3 46.9 %collective-permute-start.12 = (f32[768,8]{0,1:T(8,128)S(1)}, f32[768,8]{0,1:T(8,128)S(1)}, u32[]{:S(2)}, u32[]{:S(2)}) collective-permute-start(f32[768,8]{0,1:T(8,128)S(1)} %fusion), channel_id=1, source_target_pairs={{0,5},{1,6},{2,7},{3,8},{4,9},{5,10},{6,11},{7,12},{8,13},{9,14},{... | collective-permute-start | bytes 73736
  1248.5 46.9 %collective-permute-start.11 = (f32[768,8]{0,1:T(8,128)S(1)}, f32[768,8]{0,1:T(8,128)S(1)}, u32[]{:S(2)}, u32[]{:S(2)}) collective-permute-start(f32[768,8]{0,1:T(8,128)S(1)} %fusion), channel_id=1, source_target_pairs={{0,4},{1,5},{2,6},{3,7},{4,8},{5,9},{6,10},{7,11},{8,12},{9,13},{1... | collective-permute-start | bytes 73736
  1261.6 149.0 %collective-permute-start.6 = (bf16[192,1536]{1,0:T(8,128)(2,1)}, bf16[192,1536]{1,0:T(8,128)(2,1)}, u32[]{:S(2)}, u32[]{:S(2)}) collective-permute-start(bf16[192,1536]{1,0:T(8,128)(2,1)} %get-tuple-element.91), channel_id=1, source_target_pairs={{0,4},{4,8},{8,12},{12,16},{16,20},{20,24},{24,28},{28,32},{32,36}... | collective-permute-start | bytes 1769480 | tf_op jit(solution)/shard_map/ppermute | solution.py:29
  1265.3 145.3 %collective-permute-start.7 = (bf16[192,1536]{1,0:T(8,128)(2,1)}, bf16[192,1536]{1,0:T(8,128)(2,1)}, u32[]{:S(2)}, u32[]{:S(2)}) collective-permute-start(bf16[192,1536]{1,0:T(8,128)(2,1)} %get-tuple-element.92), channel_id=1, source_target_pairs={{4,0},{8,4},{12,8},{16,12},{20,16},{24,20},{28,24},{32,28},{36,32}... | collective-permute-start | bytes 1769480 | tf_op jit(solution)/shard_map/ppermute | solution.py:29
  1268.6 40.2 %collective-permute-start.10 = (f32[768,8]{0,1:T(8,128)S(1)}, f32[768,8]{0,1:T(8,128)S(1)}, u32[]{:S(2)}, u32[]{:S(2)}) collective-permute-start(f32[768,8]{0,1:T(8,128)S(1)} %fusion), channel_id=1, source_target_pairs={{0,3},{1,4},{2,5},{3,6},{4,7},{5,8},{6,9},{7,10},{8,11},{9,12},{10... | collective-permute-start | bytes 73736
  1282.2 26.6 %collective-permute-start.9 = (f32[768,8]{0,1:T(8,128)S(1)}, f32[768,8]{0,1:T(8,128)S(1)}, u32[]{:S(2)}, u32[]{:S(2)}) collective-permute-start(f32[768,8]{0,1:T(8,128)S(1)} %fusion), channel_id=1, source_target_pairs={{0,2},{1,3},{2,4},{3,5},{4,6},{5,7},{6,8},{7,9},{8,10},{9,11},{10,... | collective-permute-start | bytes 73736
  1295.4 20.1 %collective-permute-start.8 = (f32[768,8]{0,1:T(8,128)S(1)}, f32[768,8]{0,1:T(8,128)S(1)}, u32[]{:S(2)}, u32[]{:S(2)}) collective-permute-start(f32[768,8]{0,1:T(8,128)S(1)} %fusion), channel_id=1, source_target_pairs={{0,1},{1,2},{2,3},{3,4},{4,5},{5,6},{6,7},{7,8},{8,9},{9,10},{10,1... | collective-permute-start | bytes 73736
  (137 other events, 10550.9 us)
Sparse Core Ops, SparseCore 0:
  74.1 260.0 all-reduce.4
where the time goes:
time: 1430 us; the launch traced here: 1420 us
  blocking collectives  691 us (48%)
  starting transfers between devices  507 us (35%)
  local copies, waits for them, and re-layouts  119 us (8%)
  matrix products  40.4 us (3%)
  other arithmetic  32.6 us (2%)
  between operations  17.6 us (1%)
    unnamed x1, blocking collectives  691 us
    unnamed x65, starting transfers between devices  483 us
    unnamed x261, local copies, waits for them, and re-layouts  97.9 us
  transfers between devices with their start and end apart: 73, of which 3 were waited for; matrix products, arithmetic and copies ran while one was open for 60% of the time, Pallas kernels for 0%

commit v1 on v0

v1 whole, which is shorter than its diff:
```python
import jax
import jax.numpy as jnp
from jax import lax
from jax.experimental import pallas as pl
from jax.experimental.pallas import tpu as pltpu
from jax.sharding import PartitionSpec as P

H = 8
HD = 96
T = 192
D = 1536
W = 768
TAPS = 31
CHUNKS = D // 128
EXT = T + 32
RW = W + 128
GROUP = 4 * HD
WINDOWS = ((0, 128), (0, 256), (128, 256), (256, 128))
NEG_FILL = -1000000000.0
SCALE = HD ** (-0.5)
LOG2E = 1.4426950408889634
MESH = pl.DeviceIdType.MESH
F32 = jnp.float32
BF16 = jnp.bfloat16


def dot(a, b, ca, cb):
    return lax.dot_general(a, b, (((ca,), (cb,)), ((), ())), preferred_element_type=F32)


def window_mask(i):
    start, width = WINDOWS[i]
    lane = lax.broadcasted_iota(jnp.int32, (1, width), 1) + start
    return ((lane >= i * HD) & (lane < (i + 1) * HD)).astype(F32)


def join_heads(parts):
    lane = lax.broadcasted_iota(jnp.int32, (1, 128), 1)
    first = jnp.where(lane < 96, parts[0], parts[1][:, :128])
    second = jnp.where(lane < 64, parts[1][:, 128:], parts[2][:, :128])
    third = jnp.where(lane < 32, parts[2][:, 128:], parts[3])
    return jnp.concatenate([first, second, third], axis=1)


def lanes(c, width):
    return pl.ds(pl.multiple_of(c * width, width), width)


def kernel(
    resid_h, qkv_h, cot_h, len_s, proj_h, ker_h,
    dres_h, dqkv_h, dproj_o, dker_o,
    q_v, kv, res_v, cot_v, w_v, ker_v, probs, att_v, g_v, mext, gext, dres_v, out_v, mid,
    hs, hm, gs, hg, kt, pt, s_a, r_a, s_1, r_1, k_1, s_2, r_2, k_2, s_3, r_3,
    d_left, d_right, from_left, from_right,
    loc_sem, nb_send, nb_recv, rs_send, rs_recv,
):
    tm = lax.axis_index("tm")
    zh = lax.axis_index("dp")
    core = tm % 2
    zl = (tm // 2) % 2
    x = (tm // 4) % 4
    y = tm // 16
    other = 1 - core
    zz = zh * 2 + zl

    def device(y_, x_, zl_, core_, zh_):
        return {"tm": ((y_ * 4 + x_) * 2 + zl_) * 2 + core_, "dp": zh_}

    left = {"tm": (tm + 63) % 64, "dp": zh}
    right = {"tm": (tm + 1) % 64, "dp": zh}
    mate = device(y, x, zl, other, zh)
    first_peers = [device((y + e * other) % 4, (x + e * core) % 4, zl, core, zh) for e in (1, 2, 3)]
    second_peers = [device((y + e * core) % 4, (x + e * other) % 4, zl, core, zh) for e in (1, 2, 3)]
    z_peers = []
    for e in range(1, 8):
        z_to = (zz + e) % 8
        z_peers.append((device(y, x, z_to % 2, core, z_to // 2), (z_to % 2) * 4 + z_to // 2))

    def local(src, dst, i):
        return pltpu.make_async_copy(src, dst, loc_sem.at[i])

    def near(src, dst, i, to):
        return pltpu.make_async_remote_copy(
            src_ref=src, dst_ref=dst, send_sem=nb_send.at[i], recv_sem=nb_recv.at[i],
            device_id=to, device_id_type=MESH,
        )

    def far(src, dst, i, to):
        return pltpu.make_async_remote_copy(
            src_ref=src, dst_ref=dst, send_sem=rs_send.at[i], recv_sem=rs_recv.at[i],
            device_id=to, device_id_type=MESH,
        )

    ins = [
        local(qkv_h.at[0, :, 0:W], q_v, 0),
        local(qkv_h.at[0, :, W : 3 * W], kv.at[T : 2 * T], 1),
        local(proj_h, w_v, 2),
        local(resid_h.at[0], res_v, 3),
        local(cot_h.at[0], cot_v, 4),
        local(ker_h, ker_v, 5),
    ]
    for copy in ins:
        copy.start()

    barrier = pltpu.get_barrier_semaphore()
    everyone = [left, right] + first_peers + second_peers + [peer for peer, _ in z_peers]
    for peer in everyone:
        pl.semaphore_signal(barrier, inc=1, device_id=peer, device_id_type=MESH)
    pl.semaphore_wait(barrier, len(everyone))

    kv_copies = [
        near(qkv_h.at[0, :, W : 3 * W], kv.at[0:T], 0, right),
        near(qkv_h.at[0, :, W : 3 * W], kv.at[2 * T : 3 * T], 1, left),
    ]
    for copy in kv_copies:
        copy.start()

    length = len_s[0]
    first_frame = tm * T
    frame = first_frame + lax.broadcasted_iota(jnp.int32, (T, 1), 0)
    valid = (frame < length).astype(F32)
    key = first_frame - T + lax.broadcasted_iota(jnp.int32, (1, 3 * T), 1)
    key_open = (key >= 0) & (key < length)
    has_left = (tm > 0).astype(F32)
    has_right = (tm < 63).astype(F32)

    for copy in ins:
        copy.wait()
    for copy in kv_copies:
        copy.wait()

    def forward_group(group):
        base = group * GROUP
        outs = []
        for i in range(4):
            start, width = WINDOWS[i]
            cols = slice(base + start, base + start + width)
            v_cols = slice(W + base + start, W + base + start + width)
            q_head = q_v[:, cols] * window_mask(i).astype(BF16)
            scores = dot(q_head, kv[:, cols], 1, 1)
            scores = jnp.where(key_open, scores * (SCALE * LOG2E), NEG_FILL)
            peak = jnp.max(scores, axis=1, keepdims=True)
            weights = jnp.exp2(scores - peak)
            total = jnp.sum(weights, axis=1, keepdims=True)
            weights = (weights * (1.0 / total)).astype(BF16)
            probs[group * 4 + i] = weights
            outs.append(dot(weights, kv[:, v_cols], 1, 0))
        att_v[:, base : base + GROUP] = (join_heads(outs) * valid).astype(BF16)

    forward_group(0)
    forward_group(1)

    def project(j, carry):
        cols = lanes(j, 256)
        mixed = res_v[:, cols].astype(F32) + dot(att_v[...], w_v[:, cols], 1, 0)
        masked = (mixed.astype(BF16).astype(F32) * valid).astype(BF16)
        hs[0, :, cols] = masked[0:16]
        hs[1, :, cols] = masked[T - 16 : T]
        wide = masked.astype(F32)
        mext[2 * j, 16 : 16 + T, :] = wide[:, :128]
        mext[2 * j + 1, 16 : 16 + T, :] = wide[:, 128:]
        return carry

    lax.fori_loop(0, D // 256, project, 0)
    mask_halo = [near(hs.at[0], hm.at[1], 2, left), near(hs.at[1], hm.at[0], 3, right)]
    for copy in mask_halo:
        copy.start()

    def taps_of(c, flip):
        cols = lanes(c, 128)
        order = range(TAPS - 1, -1, -1) if flip else range(TAPS)
        return [ker_v[j : j + 1, cols] for j in order]

    def convolve(src, taps, c, row, count):
        total = taps[0] * src[c, row + 1 : row + 1 + count, :]
        for j in range(1, TAPS):
            total = total + taps[j] * src[c, row + 1 + j : row + 1 + j + count, :]
        return total

    def conv_rows(c, row, count):
        conv = convolve(mext, taps_of(c, False), c, row, count)
        sigma = jax.nn.sigmoid(conv)
        slope = sigma * (1.0 + conv * (1.0 - sigma))
        grad = (cot_v[row : row + count, lanes(c, 128)].astype(F32) * slope).astype(BF16)
        gext[c, 16 + row : 16 + row + count, :] = grad.astype(F32)
        return grad

    def back_rows(c, row, count):
        back = convolve(gext, taps_of(c, True), c, row, count)
        cot = cot_v[row : row + count, lanes(c, 128)].astype(F32)
        dres_v[row : row + count, lanes(c, 128)] = (
            cot + valid[row : row + count] * back
        ).astype(BF16)

    def conv_inner(c, carry):
        conv_rows(c, 16, 80)
        conv_rows(c, 96, 80)
        return carry

    lax.fori_loop(0, CHUNKS, conv_inner, 0)
    for copy in mask_halo:
        copy.wait()

    def conv_edge(c, carry):
        cols = lanes(c, 128)
        mext[c, 0:16, :] = hm[0, :, cols].astype(F32) * has_left
        mext[c, 16 + T : 32 + T, :] = hm[1, :, cols].astype(F32) * has_right
        gs[0, :, cols] = conv_rows(c, 0, 16)
        gs[1, :, cols] = conv_rows(c, T - 16, 16)
        return carry

    lax.fori_loop(0, CHUNKS, conv_edge, 0)
    grad_halo = [near(gs.at[0], hg.at[1], 4, left), near(gs.at[1], hg.at[0], 5, right)]
    for copy in grad_halo:
        copy.start()

    kt[...] = jnp.zeros_like(kt)

    def back_inner(c, carry):
        grad = gext[c, 16 : 16 + T, :]
        for j in range(TAPS):
            term = grad * mext[c, 1 + j : 1 + j + T, :]
            kt[j : j + 1, :] = jnp.sum(term, axis=0, keepdims=True)
        pt[lanes(c, 128), W:RW] = kt[...].T
        back_rows(c, 16, 80)
        back_rows(c, 96, 80)
        return carry

    lax.fori_loop(0, CHUNKS, back_inner, 0)
    for copy in grad_halo:
        copy.wait()

    def back_edge(c, carry):
        cols = lanes(c, 128)
        gext[c, 0:16, :] = hg[0, :, cols].astype(F32) * has_left
        gext[c, 16 + T : 32 + T, :] = hg[1, :, cols].astype(F32) * has_right
        back_rows(c, 0, 16)
        back_rows(c, T - 16, 16)
        return carry

    lax.fori_loop(0, CHUNKS, back_edge, 0)
    out_resid = local(dres_v, dres_h.at[0], 6)
    out_resid.start()

    def project_grad(j, carry):
        cols = lanes(j, 384)
        pt[cols, 0:W] = dot(dres_v[:, cols], att_v[...], 0, 0)
        return carry

    lax.fori_loop(0, 4, project_grad, 0)

    place, second = y * other + x * core, x * other + y * core

    def own_rows(a, b, which):
        y_, x_ = a * (1 - which) + b * which, b * (1 - which) + a * which
        row = (y_ * 4 + x_) * 96 + which * 24
        return jnp.concatenate(
            [
                pt[pl.ds(pl.multiple_of(row, 8), 24), :],
                pt[pl.ds(pl.multiple_of(row + 48, 8), 24), :],
            ],
            axis=0,
        )

    mate_copies = []
    for s in range(4):
        for b in range(4):
            s_a[s, b] = own_rows((second + 1 + s) % 4, b, other).astype(BF16)
        mate_copies.append(far(s_a.at[s], r_a.at[s], s, mate))
        mate_copies[-1].start()

    def attended_grad(j, carry):
        cols = lanes(j, 256)
        g_v[:, cols] = (valid * dot(dres_v[...], w_v[cols, :], 1, 1)).astype(BF16)
        return carry

    lax.fori_loop(0, W // 256, attended_grad, 0)

    def backward_group(group):
        base = group * GROUP
        d_q, d_k, d_v = [], [], []
        for i in range(4):
            start, width = WINDOWS[i]
            cols = slice(base + start, base + start + width)
            v_cols = slice(W + base + start, W + base + start + width)
            g_win = g_v[:, cols]
            g_head = g_win * window_mask(i).astype(BF16)
            delta = jnp.sum(
                g_head.astype(F32) * att_v[:, cols].astype(F32), axis=1, keepdims=True
            )
            slopes = dot(g_head, kv[:, v_cols], 1, 1)
            weights = probs[group * 4 + i]
            dscore = (weights.astype(F32) * ((slopes - delta) * SCALE)).astype(BF16)
            d_q.append(dot(dscore, kv[:, cols], 1, 0))
            d_k.append(dot(dscore, q_v[:, cols], 0, 0))
            d_v.append(dot(weights, g_win, 0, 0))
        out_v[:, base : base + GROUP] = join_heads(d_q).astype(BF16)
        for part, grads in enumerate((d_k, d_v)):
            whole = join_heads(grads)
            cols = slice(part * GROUP, (part + 1) * GROUP)
            d_left[group, :, cols] = whole[0:T].astype(BF16)
            mid[group, :, cols] = whole[T : 2 * T]
            d_right[group, :, cols] = whole[2 * T : 3 * T].astype(BF16)
        copies = [
            near(d_left.at[group], from_right.at[group], 6 + 2 * group, left),
            near(d_right.at[group], from_left.at[group], 7 + 2 * group, right),
        ]
        for copy in copies:
            copy.start()
        return copies

    first_copies = []
    for s in range(4):
        a = (place + 1 + s) % 4
        mate_copies[s].wait()
        for b in range(4):
            total = own_rows(a, b, core) + r_a[s, b].astype(F32)
            if s < 3:
                s_1[s, b] = total.astype(BF16)
            else:
                k_1[b] = total
        if s < 3:
            first_copies.append(far(s_1.at[s], r_1.at[s], 4 + s, first_peers[s]))
            first_copies[-1].start()

    pair_copies = backward_group(0)

    for copy in first_copies:
        copy.wait()
    second_copies = []
    for s in range(4):
        b = (second + 1 + s) % 4
        total = k_1[b]
        for e in range(3):
            total = total + r_1[e, b].astype(F32)
        if s < 3:
            s_2[s] = total.astype(BF16)
            second_copies.append(far(s_2.at[s], r_2.at[s], 7 + s, second_peers[s]))
            second_copies[-1].start()
        else:
            k_2[...] = total

    pair_copies += backward_group(1)

    for copy in second_copies:
        copy.wait()
    total = k_2[...]
    for e in range(3):
        total = total + r_2[e].astype(F32)
    s_3[...] = jnp.zeros_like(s_3)
    for part in range(8):
        s_3[part, 0:6, :] = total[part * 6 : part * 6 + 6]
    z_copies = []
    for e, (peer, part) in enumerate(z_peers):
        z_copies.append(far(s_3.at[part], r_3.at[e], 10 + e, peer))
        z_copies[-1].start()

    for copy in pair_copies:
        copy.wait()
    for group in range(2):
        for part in range(2):
            cols = slice(part * GROUP, (part + 1) * GROUP)
            whole = (
                mid[group, :, cols]
                + from_left[group, :, cols].astype(F32)
                + from_right[group, :, cols].astype(F32)
            )
            start = (1 + part) * W + group * GROUP
            out_v[:, start : start + GROUP] = whole.astype(BF16)
    out_qkv = local(out_v, dqkv_h.at[0], 7)
    out_qkv.start()

    for copy in z_copies:
        copy.wait()
    total = s_3[zl * 4 + zh]
    for e in range(7):
        total = total + r_3[e]
    turned = jnp.concatenate([total, jnp.zeros((120, RW), F32)], axis=0).T
    dproj_o[...] = turned[0:W, 0:6]
    dker_o[...] = turned[W : W + TAPS, 0:6]
    out_resid.wait()
    out_qkv.wait()


def local(resid, qkv, cotangent, lengths, out_proj, ker):
    hbm = pl.BlockSpec(memory_space=pl.ANY)
    vmem = pl.BlockSpec(memory_space=pltpu.VMEM)
    scratch = [
        ((T, W), BF16), ((3 * T, 2 * W), BF16), ((T, D), BF16), ((T, D), BF16),
        ((W, D), BF16), ((TAPS, D), F32), ((H, T, 3 * T), BF16), ((T, W), BF16),
        ((T, W), BF16), ((CHUNKS, EXT, 128), F32), ((CHUNKS, EXT, 128), F32), ((T, D), BF16),
        ((T, 3 * W), BF16), ((2, T, 2 * GROUP), F32),
        ((2, 16, D), BF16), ((2, 16, D), BF16), ((2, 16, D), BF16), ((2, 16, D), BF16),
        ((128, 128), F32), ((D, RW), F32),
        ((4, 4, 48, RW), BF16), ((4, 4, 48, RW), BF16),
        ((3, 4, 48, RW), BF16), ((3, 4, 48, RW), BF16), ((4, 48, RW), F32),
        ((3, 48, RW), BF16), ((3, 48, RW), BF16), ((48, RW), F32),
        ((8, 8, RW), F32), ((7, 8, RW), F32),
        ((2, T, 2 * GROUP), BF16), ((2, T, 2 * GROUP), BF16),
        ((2, T, 2 * GROUP), BF16), ((2, T, 2 * GROUP), BF16),
    ]
    return pl.pallas_call(
        kernel,
        out_shape=[
            jax.ShapeDtypeStruct((1, T, D), BF16),
            jax.ShapeDtypeStruct((1, T, 3 * W), BF16),
            jax.ShapeDtypeStruct((W, 6), F32),
            jax.ShapeDtypeStruct((TAPS, 6), F32),
        ],
        in_specs=[hbm, hbm, hbm, pl.BlockSpec(memory_space=pltpu.SMEM), hbm, hbm],
        out_specs=[hbm, hbm, vmem, vmem],
        scratch_shapes=[pltpu.VMEM(shape, kind) for shape, kind in scratch]
        + [
            pltpu.SemaphoreType.DMA((8,)),
            pltpu.SemaphoreType.DMA((10,)),
            pltpu.SemaphoreType.DMA((10,)),
            pltpu.SemaphoreType.DMA((17,)),
            pltpu.SemaphoreType.DMA((17,)),
        ],
        compiler_params=pltpu.CompilerParams(
            collective_id=0, has_side_effects=True, vmem_limit_bytes=56 * 2**20
        ),
        cost_estimate=pl.CostEstimate(
            flops=3_000_000_000, bytes_accessed=8_000_000, transcendentals=1_000_000
        ),
    )(resid, qkv, cotangent, lengths, out_proj, ker)


def solution(mesh):
    in_specs = (P("dp", "tm", None), P("dp", "tm", None), P("dp", "tm", None), P("dp"), P(), P())
    out_specs = (
        P("dp", "tm", None),
        P("dp", "tm", None),
        P(None, ("tm", "dp")),
        P(None, ("tm", "dp")),
    )
    return jax.shard_map(local, mesh=mesh, in_specs=in_specs, out_specs=out_specs, check_vma=False)
```

time: 1430 us -> 79.9 us (0.06)
  blocking collectives: 691 us -> 0 us
  starting transfers between devices: 507 us -> 0 us
  local copies, waits for them, and re-layouts: 119 us -> 7.19 us
  Pallas kernels: 0 us -> 70.6 us
  matrix products: 40.4 us -> 0 us
  other arithmetic: 32.6 us -> 0 us
  between operations: 17.6 us -> 1.29 us
    unnamed x1 -> x0, blocking collectives: 691 us -> none
    unnamed x65 -> x0, starting transfers between devices: 483 us -> none
    unnamed x261 -> x2, local copies, waits for them, and re-layouts: 97.9 us -> 4.05 us
    pallas_call x0 -> x1, Pallas kernels: none -> 70.6 us  [local(): pl.pallas_call(kernel, out_shape=[jax.ShapeDtypeStruct((1, T, D), BF16),...]
    dot_general x51 -> x0, matrix products: 40.4 us -> none  [the longest x8 9.15 us: grad_heads(): lax.dot_general(dscore, q_head, (((0,), (0,)), ((), ())), preferred_eleme...]
    ppermute x8 -> x0, starting transfers between devices: 24.1 us -> none  [the longest x3 9.07 us: padded(): lax.ppermute(lax.slice_in_dim(block, block.shape[dim] - width, None, axis...]
    reduce_sum x13 -> x0, other arithmetic: 18 us -> none  [the longest x4 14.7 us: local(): jnp.sum(conv_grad_wide * masked_rim[tap_index:tap_index + shard_rows].ast...]
  transfers between devices with their start and end apart: 73 -> 0, of which waited for: 3 -> 0; matrix products, arithmetic and copies ran while one was open for 60% -> 0% of each run, Pallas kernels for 0% -> 0%
where the time goes in v1:
time: 79.9 us; the launch traced here: 79.1 us
  Pallas kernels  70.6 us (88%)
  local copies, waits for them, and re-layouts  7.19 us (9%)
  between operations  1.29 us (2%)
    pallas_call x1, Pallas kernels, local(): pl.pallas_call(kernel, out_shape=[jax.ShapeDtypeStruct((1, T, D), BF16),...  70.6 us
    unnamed x2, local copies, waits for them, and re-layouts  4.05 us
    pallas_call x2, local copies, waits for them, and re-layouts, local(): pl.pallas_call(kernel, out_shape=[jax.ShapeDtypeStruct((1, T, D), BF16),...  3.14 us

profile of v1, /device:TPU:1, one launch (start us, length us, event | category | flops | bytes accessed | tf_op | source)
XLA Modules:
  0.0 79.1 jit_solution(4217164986250986505)
XLA Ops:
  1.3 70.6 %shard_map.93 = (bf16[1,192,1536]{2,1,0:T(8,128)(2,1)}, bf16[1,192,2304]{2,1,0:T(8,128)(2,1)}, f32[768,6]{1,0:T(8,128)}, f32[31,6]{1,0:T(8,128)}) custom-call(bf16[1,192,1536]{2,1,0:T(8,128)(2,1)} %resid_h.1, bf16[1,192,2304]{2,1,0:T(8,128)(2,1)} %qkv_h.1, bf16[1,192,1536]{2,1,0:T(8,128)(2,1)} %cot_h.1, s32[1]{0:T(128)S(6)} %copy.14.len_s, ...), custom_call_target="tpu_custom_call" | custom-call | flops 3000000000 | bytes 8000000 | tf_op jit(solution)/shard_map/pallas_call | solution.py:402
  71.9 1.4 %copy.11 = f32[31,6]{0,1:T(8,128)} copy(f32[31,6]{1,0:T(8,128)} %get-tuple-element.7) | data formatting | bytes 1488 | tf_op jit(solution)/shard_map/pallas_call | solution.py:402
  73.3 1.8 %copy.10 = f32[768,6]{0,1:T(8,128)} copy(f32[768,6]{1,0:T(8,128)} %get-tuple-element.6) | data formatting | bytes 36864 | tf_op jit(solution)/shard_map/pallas_call | solution.py:402
  75.0 1.9 %copy.15 = bf16[1,192,1536]{2,1,0:T(8,128)(2,1)} copy(bf16[1,192,1536]{2,1,0:T(8,128)(2,1)} %get-tuple-element.12) | data formatting | bytes 1179648
  76.9 2.1 %copy.16 = bf16[1,192,2304]{2,1,0:T(8,128)(2,1)} copy(bf16[1,192,2304]{2,1,0:T(8,128)(2,1)} %get-tuple-element.13) | data formatting | bytes 1769472

commit v2 on v1

v2 whole, which is shorter than its diff:
```python
import jax
import jax.numpy as jnp
from jax import lax
from jax.experimental import pallas as pl
from jax.experimental.pallas import tpu as pltpu
from jax.sharding import PartitionSpec as P

H = 8
HD = 96
T = 192
D = 1536
W = 768
TAPS = 31
CHUNKS = D // 128
EDGE = 16
REACH = 2 * EDGE
RW = W + 128
KEYS = 3 * T
GROUP = 4 * HD
WINDOWS = ((0, 128), (0, 256), (128, 256), (256, 128))
NEG_FILL = -1000000000.0
SCALE = HD ** (-0.5)
LOG2E = 1.4426950408889634
MESH = pl.DeviceIdType.MESH
F32 = jnp.float32
BF16 = jnp.bfloat16


def dot(a, b, ca, cb):
    return lax.dot_general(a, b, (((ca,), (cb,)), ((), ())), preferred_element_type=F32)


def window_mask(i):
    start, width = WINDOWS[i]
    lane = lax.broadcasted_iota(jnp.int32, (1, width), 1) + start
    return ((lane >= i * HD) & (lane < (i + 1) * HD)).astype(F32)


def join_heads(parts):
    lane = lax.broadcasted_iota(jnp.int32, (1, 128), 1)
    first = jnp.where(lane < 96, parts[0], parts[1][:, :128])
    second = jnp.where(lane < 64, parts[1][:, 128:], parts[2][:, :128])
    third = jnp.where(lane < 32, parts[2][:, 128:], parts[3])
    return jnp.concatenate([first, second, third], axis=1)


def lanes(c, width):
    return pl.ds(pl.multiple_of(c * width, width), width)


def kernel(
    resid_h, qkv_h, cot_h, len_s, proj_h, ker_h,
    dres_h, dqkv_h, sums_o,
    q_all, kv, res_v, cot_v, w_v, ker_v, probs, probs_k, stat, att_v, att_m, go,
    mext, gext, dres_v, out_v, hs, hm, hc, kt, kt_part, kt_all, turned, lhs_own, lhs_out, lhs_in,
    s_2hop, r_2hop, s_up, s_down, keep_up, keep_down, r_up, r_down, own_1,
    s_2, r_2, own_2, s_3, r_3,
    loc_sem, nb_send, nb_recv, rs_send, rs_recv,
):
    tm = lax.axis_index("tm")
    zh = lax.axis_index("dp")
    core = tm % 2
    zl = (tm // 2) % 2
    x = (tm // 4) % 4
    y = tm // 16
    other = 1 - core
    zz = zh * 2 + zl

    def device(y_, x_, zl_, core_, zh_):
        return {"tm": ((y_ * 4 + x_) * 2 + zl_) * 2 + core_, "dp": zh_}

    left = {"tm": (tm + 63) % 64, "dp": zh}
    right = {"tm": (tm + 1) % 64, "dp": zh}
    mate = device(y, x, zl, other, zh)
    up = device((y + other) % 4, (x + core) % 4, zl, core, zh)
    down = device((y + 3 * other) % 4, (x + 3 * core) % 4, zl, core, zh)
    second_peers = [device((y + e * core) % 4, (x + e * other) % 4, zl, core, zh) for e in (1, 2, 3)]
    z_peers = []
    for e in range(1, 8):
        z_to = (zz + e) % 8
        z_peers.append((device(y, x, z_to % 2, core, z_to // 2), (z_to % 2) * 4 + z_to // 2))

    def local(src, dst, i):
        return pltpu.make_async_copy(src, dst, loc_sem.at[i])

    def near(src, dst, i, to):
        return pltpu.make_async_remote_copy(
            src_ref=src, dst_ref=dst, send_sem=nb_send.at[i], recv_sem=nb_recv.at[i],
            device_id=to, device_id_type=MESH,
        )

    def far(src, dst, i, to):
        return pltpu.make_async_remote_copy(
            src_ref=src, dst_ref=dst, send_sem=rs_send.at[i], recv_sem=rs_recv.at[i],
            device_id=to, device_id_type=MESH,
        )

    def start(copies):
        for copy in copies:
            copy.start()
        return copies

    def wait(copies):
        for copy in copies:
            copy.wait()

    low, own, high = slice(0, T), slice(T, 2 * T), slice(2 * T, 3 * T)

    ins = start([
        local(qkv_h.at[0, :, 0:W], q_all.at[own], 0),
        local(qkv_h.at[0, :, W : 3 * W], kv.at[own], 1),
        local(proj_h, w_v, 2),
        local(resid_h.at[0], res_v, 3),
        local(cot_h.at[0], cot_v, 4),
        local(ker_h, ker_v, 5),
    ])

    barrier = pltpu.get_barrier_semaphore()
    everyone = [left, right, up, down] + second_peers + [peer for peer, _ in z_peers]
    for peer in everyone:
        pl.semaphore_signal(barrier, inc=1, device_id=peer, device_id_type=MESH)
    pl.semaphore_wait(barrier, len(everyone))

    kv_copies = []
    for group in range(2):
        for part in range(2):
            cols = slice(part * W + group * GROUP, part * W + (group + 1) * GROUP)
            src = qkv_h.at[0, :, W + cols.start : W + cols.stop]
            i = group * 4 + part * 2
            kv_copies.append(near(src, kv.at[low, cols], i, right))
            kv_copies.append(near(src, kv.at[high, cols], i + 1, left))
    start(kv_copies)

    length = len_s[0]
    first_frame = tm * T
    frame = first_frame + lax.broadcasted_iota(jnp.int32, (T, 1), 0)
    valid = (frame < length).astype(F32)
    key = first_frame - T + lax.broadcasted_iota(jnp.int32, (1, KEYS), 1)
    key_open = (key >= 0) & (key < length)
    own_key = first_frame + lax.broadcasted_iota(jnp.int32, (1, T), 1)
    near_query = first_frame - T + lax.broadcasted_iota(jnp.int32, (KEYS, 1), 0)
    pair_open = (own_key < length) & (near_query >= 0) & (near_query < 64 * T)
    has_left = (tm > 0).astype(F32)
    has_right = (tm < 63).astype(F32)
    lane = lax.broadcasted_iota(jnp.int32, (1, 128), 1)

    kt[...] = jnp.zeros_like(kt)
    att_v[T:256, :] = jnp.zeros((256 - T, W), BF16)
    s_3[...] = jnp.zeros_like(s_3)

    wait(ins)
    wait(kv_copies[:4])

    def forward_group(group, stats):
        base = group * GROUP
        outs = []
        for i in range(4):
            start_, width = WINDOWS[i]
            cols = slice(base + start_, base + start_ + width)
            v_cols = slice(W + base + start_, W + base + start_ + width)
            q_head = q_all[own, cols] * window_mask(i).astype(BF16)
            scores = dot(q_head, kv[:, cols], 1, 1)
            scores = jnp.where(key_open, scores * (SCALE * LOG2E), NEG_FILL)
            peak = jnp.max(scores, axis=1, keepdims=True)
            weights = jnp.exp2(scores - peak)
            total = jnp.sum(weights, axis=1, keepdims=True)
            weights = (weights * (1.0 / total)).astype(BF16)
            probs[group * 4 + i] = weights
            stats = jnp.where(lane == group * 4 + i, peak + jnp.log2(total), stats)
            outs.append(dot(weights, kv[:, v_cols], 1, 0))
        att_v[0:T, base : base + GROUP] = (join_heads(outs) * valid).astype(BF16)
        return stats

    stats = forward_group(0, jnp.zeros((T, 128), F32))
    wait(kv_copies[4:])
    early = start([
        near(cot_v.at[0:EDGE], hc.at[1], 8, left),
        near(cot_v.at[T - EDGE : T], hc.at[0], 9, right),
    ])
    q_copies = start([
        near(q_all.at[own, 0:GROUP], q_all.at[low, 0:GROUP], 10, right),
        near(q_all.at[own, 0:GROUP], q_all.at[high, 0:GROUP], 11, left),
    ])
    stat[own, :] = forward_group(1, stats)
    early += start([far(att_v, att_m, 0, mate)])

    def project(j, carry):
        cols = lanes(j, 256)
        mixed = res_v[:, cols].astype(F32) + dot(att_v[0:T, :], w_v[:, cols], 1, 0)
        masked = (mixed.astype(BF16).astype(F32) * valid).astype(BF16)
        hs[0, :, cols] = masked[0:REACH]
        hs[1, :, cols] = masked[T - REACH : T]
        wide = masked.astype(F32)
        mext[2 * j, REACH : REACH + T, :] = wide[:, :128]
        mext[2 * j + 1, REACH : REACH + T, :] = wide[:, 128:]
        return carry

    lax.fori_loop(0, D // 256, project, 0)
    mask_halo = start([near(hs.at[0], hm.at[1], 12, left), near(hs.at[1], hm.at[0], 13, right)])

    def windows(src, c, first, count):
        for s in range(8):
            taps = range(s, TAPS, 8)
            window = src[c, first + s : first + s + count + 8 * (len(taps) - 1), :]
            for place, j in enumerate(taps):
                yield j, window[8 * place : 8 * place + count]

    def convolve(src, c, first, count, flip):
        total = None
        for j, rows in windows(src, c, first, count):
            tap = TAPS - 1 - j if flip else j
            term = ker_v[tap : tap + 1, lanes(c, 128)] * rows
            total = term if total is None else total + term
        return total

    def conv_rows(c, row, count, cot):
        conv = convolve(mext, c, row + REACH - 15, count, False)
        sigma = jax.nn.sigmoid(conv)
        slope = sigma * (1.0 + conv * (1.0 - sigma))
        grad = (cot * slope).astype(BF16).astype(F32)
        gext[c, EDGE + row : EDGE + row + count, :] = grad

    def back_rows(c, row, count):
        cols = lanes(c, 128)
        back = convolve(gext, c, row + EDGE - 15, count, True)
        cot = cot_v[row : row + count, cols].astype(F32)
        dres_v[row : row + count, cols] = (cot + valid[row : row + count] * back).astype(BF16)

    def kernel_terms(c, row, count, sums):
        grad = gext[c, EDGE + row : EDGE + row + count, :]
        for j, rows in windows(mext, c, row + REACH - 15, count):
            term = jnp.sum((grad * rows).reshape(count // 8, 8, 128), axis=0)
            sums[j] = term if sums[j] is None else sums[j] + term

    def conv_inner(c, carry):
        for row in (16, 96):
            conv_rows(c, row, 80, cot_v[row : row + 80, lanes(c, 128)].astype(F32))
        sums = [None] * TAPS
        for row in (16, 96):
            kernel_terms(c, row, 80, sums)
        for j in range(TAPS):
            kt_part[c, 8 * j : 8 * j + 8, :] = sums[j]
        return carry

    lax.fori_loop(0, CHUNKS // 2, conv_inner, 0)
    q_copies += start([
        near(q_all.at[own, GROUP:W], q_all.at[low, GROUP:W], 14, right),
        near(q_all.at[own, GROUP:W], q_all.at[high, GROUP:W], 15, left),
        near(stat.at[own], stat.at[low], 16, right),
        near(stat.at[own], stat.at[high], 17, left),
    ])
    lax.fori_loop(CHUNKS // 2, CHUNKS, conv_inner, 0)
    wait(early)
    wait(mask_halo)

    def edges_and_back(c, carry):
        cols = lanes(c, 128)
        mext[c, 0:REACH, :] = hm[0, :, cols].astype(F32) * has_left
        mext[c, REACH + T : 2 * REACH + T, :] = hm[1, :, cols].astype(F32) * has_right
        cot = cot_v[0:EDGE, cols].astype(F32)
        before = hc[0, :, cols].astype(F32) * has_left
        conv_rows(c, -EDGE, REACH, jnp.concatenate([before, cot], axis=0))
        cot = cot_v[T - EDGE : T, cols].astype(F32)
        after = hc[1, :, cols].astype(F32) * has_right
        conv_rows(c, T - EDGE, REACH, jnp.concatenate([cot, after], axis=0))
        sums = [kt_part[c, 8 * j : 8 * j + 8, :] for j in range(TAPS)]
        kernel_terms(c, 0, EDGE, sums)
        kernel_terms(c, T - EDGE, EDGE, sums)
        for j in range(TAPS):
            kt[j : j + 1, :] = jnp.sum(sums[j], axis=0, keepdims=True)
        kt_all[cols, :] = kt[...].T
        back_rows(c, 0, 96)
        back_rows(c, 96, 96)
        grad = dres_v[:, cols].astype(F32)
        turned[cols, :] = jnp.concatenate([grad, jnp.zeros((256 - T, 128), F32)], axis=0).T
        return carry

    def rows_of(ref, block, which):
        row = block * 96 + which * 24
        return jnp.concatenate(
            [
                ref[pl.ds(pl.multiple_of(row, 8), 24), :],
                ref[pl.ds(pl.multiple_of(row + 48, 8), 24), :],
            ],
            axis=0,
        )

    pair_copies = []
    for quarter in range(4):
        lax.fori_loop(3 * quarter, 3 * quarter + 3, edges_and_back, 0)
        for block in range(4 * quarter, 4 * quarter + 4):
            lhs_out[block, :, 0:256] = rows_of(turned, block, other).astype(BF16)
            lhs_out[block, :, 256:384] = rows_of(kt_all, block, other).astype(BF16)
        quarters = slice(4 * quarter, 4 * quarter + 4)
        pair_copies += start([far(lhs_out.at[quarters], lhs_in.at[quarters], 15 + quarter, mate)])
    out_resid = start([local(dres_v, dres_h.at[0], 6)])

    place, second = y * other + x * core, x * other + y * core

    def attended_grad(j, carry):
        go[own, pl.ds(pl.multiple_of(128 + j * 256, 128), 256)] = (
            valid * dot(dres_v[...], w_v[lanes(j, 256), :], 1, 1)
        ).astype(BF16)
        return carry

    lax.fori_loop(0, W // 256, attended_grad, 0)
    deltas = jnp.zeros((T, 128), F32)
    for head in range(H):
        start_, width = WINDOWS[head % 4]
        first = head // 4 * GROUP + start_
        product = (
            go[own, 128 + first : 128 + first + width].astype(F32)
            * att_v[0:T, first : first + width].astype(F32)
        )
        delta = jnp.sum(product * window_mask(head % 4), axis=1, keepdims=True)
        coarse = delta.astype(BF16).astype(F32)
        deltas = jnp.where(lane == head, coarse, deltas)
        deltas = jnp.where(lane == H + head, delta - coarse, deltas)
    go[own, 0:128] = deltas.astype(BF16)
    first, last = slice(0, 128 + GROUP), slice(128 + GROUP, 128 + W)

    def send_grads(cols, i):
        return start([
            near(go.at[own, cols], go.at[low, cols], i, right),
            near(go.at[own, cols], go.at[high, cols], i + 1, left),
        ])

    grad_copies = [send_grads(first, 18)]

    def gather_own(block, carry):
        lhs_own[block] = rows_of(turned, block, core).astype(BF16)
        return carry

    lax.fori_loop(0, 16, gather_own, 0)
    wait(pair_copies)

    def pair_sum(a):
        blocks = [(a * other + b * core) * 4 + b * other + a * core for b in range(4)]
        mine = jnp.concatenate([lhs_own[block] for block in blocks], axis=0)
        theirs = jnp.concatenate([lhs_in[block, :, 0:256] for block in blocks], axis=0)
        main = dot(mine, att_v[...], 1, 0) + dot(theirs, att_m[...], 1, 0)
        side = jnp.concatenate(
            [
                rows_of(kt_all, block, core) + lhs_in[block, :, 256:384].astype(F32)
                for block in blocks
            ],
            axis=0,
        )
        return jnp.concatenate([main, side], axis=1)

    half = 96
    whole = pair_sum((place + 2) % 4)
    s_2hop[0:half] = whole[0:half].astype(BF16)
    s_2hop[half:T] = whole[half:T].astype(BF16)
    two_hop = start([
        far(s_2hop.at[0:half], r_2hop.at[0:half], 1, up),
        far(s_2hop.at[half:T], r_2hop.at[half:T], 2, down),
    ])
    whole = pair_sum((place + 1) % 4)
    keep_up[...] = whole[0:half]
    s_up[half:T] = whole[half:T].astype(BF16)
    one_hop = start([far(s_up.at[half:T], r_up.at[half:T], 3, up)])
    whole = pair_sum((place + 3) % 4)
    s_down[0:half] = whole[0:half].astype(BF16)
    keep_down[...] = whole[half:T]
    one_hop += start([far(s_down.at[0:half], r_down.at[0:half], 4, down)])
    own_1[...] = pair_sum(place)

    def query_group(group):
        base = group * GROUP
        d_q = []
        for i in range(4):
            head = group * 4 + i
            start_, width = WINDOWS[i]
            cols = slice(base + start_, base + start_ + width)
            v_cols = slice(W + base + start_, W + base + start_ + width)
            g_cols = slice(128 + base + start_, 128 + base + start_ + width)
            g_head = go[own, g_cols] * window_mask(i).astype(BF16)
            delta = go[own, head : head + 1].astype(F32) + go[own, H + head : H + head + 1].astype(F32)
            slopes = dot(g_head, kv[:, v_cols], 1, 1)
            dscore = (probs[head].astype(F32) * ((slopes - delta) * SCALE)).astype(BF16)
            d_q.append(dot(dscore, kv[:, cols], 1, 0))
        out_v[:, base : base + GROUP] = join_heads(d_q).astype(BF16)

    def probs_group(group):
        base = group * GROUP
        for i in range(4):
            head = group * 4 + i
            start_, width = WINDOWS[i]
            cols = slice(base + start_, base + start_ + width)
            k_head = kv[own, cols] * window_mask(i).astype(BF16)
            scores = dot(q_all[:, cols], k_head, 1, 1)
            scores = jnp.where(pair_open, scores * (SCALE * LOG2E), NEG_FILL)
            probs_k[head] = jnp.exp2(scores - stat[:, head : head + 1]).astype(BF16)

    def key_group(group):
        base = group * GROUP
        d_k, d_v = [], []
        for i in range(4):
            head = group * 4 + i
            start_, width = WINDOWS[i]
            cols = slice(base + start_, base + start_ + width)
            v_cols = slice(W + base + start_, W + base + start_ + width)
            g_win = go[:, 128 + base + start_ : 128 + base + start_ + width]
            v_head = kv[own, v_cols] * window_mask(i).astype(BF16)
            delta = go[:, head : head + 1].astype(F32) + go[:, H + head : H + head + 1].astype(F32)
            slopes = dot(g_win, v_head, 1, 1)
            weights = probs_k[head]
            dscore = (weights.astype(F32) * ((slopes - delta) * SCALE)).astype(BF16)
            d_k.append(dot(dscore, q_all[:, cols], 0, 0))
            d_v.append(dot(weights, g_win, 0, 0))
        out_v[:, W + base : W + base + GROUP] = join_heads(d_k).astype(BF16)
        out_v[:, 2 * W + base : 2 * W + base + GROUP] = join_heads(d_v).astype(BF16)

    query_group(0)
    wait(two_hop)
    s_up[0:half] = (keep_up[...] + r_2hop[0:half].astype(F32)).astype(BF16)
    one_hop += start([far(s_up.at[0:half], r_up.at[0:half], 5, up)])
    s_down[half:T] = (keep_down[...] + r_2hop[half:T].astype(F32)).astype(BF16)
    one_hop += start([far(s_down.at[half:T], r_down.at[half:T], 6, down)])

    query_group(1)
    wait(q_copies)
    probs_group(0)
    probs_group(1)

    wait(one_hop)
    grad_copies.append(send_grads(last, 20))
    second_copies = []
    for s in range(4):
        rows = pl.ds(pl.multiple_of((second + 1 + s) % 4 * 48, 16), 48)
        total = own_1[rows, :] + r_up[rows, :].astype(F32) + r_down[rows, :].astype(F32)
        if s < 3:
            s_2[s] = total.astype(BF16)
            second_copies += start([far(s_2.at[s], r_2.at[s], 7 + s, second_peers[s])])
        else:
            own_2[...] = total

    wait(grad_copies[0])
    key_group(0)

    wait(second_copies)
    total = own_2[...]
    for e in range(3):
        total = total + r_2[e].astype(F32)
    for part in range(8):
        s_3[part, 0:6, :] = total[part * 6 : part * 6 + 6]
    z_copies = []
    for e, (peer, part) in enumerate(z_peers):
        z_copies += start([far(s_3.at[part], r_3.at[e], 19 + e, peer)])

    wait(grad_copies[1])
    key_group(1)
    out_qkv = start([local(out_v, dqkv_h.at[0], 7)])

    wait(z_copies)
    total = s_3[zl * 4 + zh]
    for e in range(7):
        total = total + r_3[e]
    sums_o[...] = total
    wait(out_resid)
    wait(out_qkv)


def hand_over(dres_i, dqkv_i, sums_i, dres_o, dqkv_o, dproj_o, dker_o, sem):
    copies = [
        pltpu.make_async_copy(dres_i, dres_o, sem.at[0]),
        pltpu.make_async_copy(dqkv_i, dqkv_o, sem.at[1]),
    ]
    for copy in copies:
        copy.start()
    dproj_o[...] = sums_i[0:6, 0:W]
    dker_o[...] = sums_i[0:6, W : W + TAPS]
    for copy in copies:
        copy.wait()


def local(resid, qkv, cotangent, lengths, out_proj, ker):
    hbm = pl.BlockSpec(memory_space=pl.ANY)
    vmem = pl.BlockSpec(memory_space=pltpu.VMEM)
    scratch = [
        ((KEYS, W), BF16), ((KEYS, 2 * W), BF16), ((T, D), BF16), ((T, D), BF16),
        ((W, D), BF16), ((TAPS, D), F32), ((H, T, KEYS), BF16), ((H, KEYS, T), BF16),
        ((KEYS, 128), F32), ((256, W), BF16), ((256, W), BF16), ((KEYS, RW), BF16),
        ((CHUNKS, T + 2 * REACH, 128), F32), ((CHUNKS, T + 2 * EDGE, 128), F32), ((T, D), BF16),
        ((T, 3 * W), BF16),
        ((2, REACH, D), BF16), ((2, REACH, D), BF16), ((2, EDGE, D), BF16),
        ((128, 128), F32), ((CHUNKS, 8 * TAPS, 128), F32), ((D, 128), F32), ((D, 256), F32),
        ((16, 48, 256), BF16), ((16, 48, 384), BF16), ((16, 48, 384), BF16),
        ((T, RW), BF16), ((T, RW), BF16), ((T, RW), BF16), ((T, RW), BF16),
        ((T // 2, RW), F32), ((T // 2, RW), F32), ((T, RW), BF16), ((T, RW), BF16),
        ((T, RW), F32),
        ((3, 48, RW), BF16), ((3, 48, RW), BF16), ((48, RW), F32),
        ((8, 8, RW), F32), ((7, 8, RW), F32),
    ]
    dres, dqkv, sums = pl.pallas_call(
        kernel,
        out_shape=[
            jax.ShapeDtypeStruct((1, T, D), BF16),
            jax.ShapeDtypeStruct((1, T, 3 * W), BF16),
            jax.ShapeDtypeStruct((8, RW), F32),
        ],
        in_specs=[hbm, hbm, hbm, pl.BlockSpec(memory_space=pltpu.SMEM), hbm, hbm],
        out_specs=[hbm, hbm, vmem],
        scratch_shapes=[pltpu.VMEM(shape, kind) for shape, kind in scratch]
        + [
            pltpu.SemaphoreType.DMA((8,)),
            pltpu.SemaphoreType.DMA((22,)),
            pltpu.SemaphoreType.DMA((22,)),
            pltpu.SemaphoreType.DMA((26,)),
            pltpu.SemaphoreType.DMA((26,)),
        ],
        compiler_params=pltpu.CompilerParams(
            collective_id=0, has_side_effects=True, vmem_limit_bytes=56 * 2**20
        ),
        cost_estimate=pl.CostEstimate(
            flops=3_000_000_000, bytes_accessed=8_000_000, transcendentals=1_000_000
        ),
    )(resid, qkv, cotangent, lengths, out_proj, ker)
    dres, dqkv, dproj, dker = pl.pallas_call(
        hand_over,
        out_shape=[
            jax.ShapeDtypeStruct((1, T, D), BF16),
            jax.ShapeDtypeStruct((1, T, 3 * W), BF16),
            jax.ShapeDtypeStruct((6, W), F32),
            jax.ShapeDtypeStruct((6, TAPS), F32),
        ],
        in_specs=[vmem, vmem, vmem],
        out_specs=[hbm, hbm, vmem, vmem],
        scratch_shapes=[pltpu.SemaphoreType.DMA((2,))],
        cost_estimate=pl.CostEstimate(flops=0, bytes_accessed=4_000_000, transcendentals=0),
    )(dres, dqkv, sums)
    return dres, dqkv, dproj.T, dker.T


def solution(mesh):
    in_specs = (P("dp", "tm", None), P("dp", "tm", None), P("dp", "tm", None), P("dp"), P(), P())
    out_specs = (
        P("dp", "tm", None),
        P("dp", "tm", None),
        P(None, ("tm", "dp")),
        P(None, ("tm", "dp")),
    )
    return jax.shard_map(local, mesh=mesh, in_specs=in_specs, out_specs=out_specs, check_vma=False)
```

time: 79.9 us -> 71 us (0.89)
  the two profiles are of different devices: /device:TPU:1 before, /device:TPU:39 now
where the time goes in v2:
time: 71 us; the launch traced here: 70.9 us
  Pallas kernels  69.4 us (98%)
  between operations  1.45 us (2%)
    pallas_call x1, Pallas kernels, local(): pl.pallas_call(kernel, out_shape=[jax.ShapeDtypeStruct((1, T, D), BF16),...  66.4 us
    pallas_call x1, Pallas kernels, local(): pl.pallas_call(hand_over, out_shape=[jax.ShapeDtypeStruct((1, T, D), BF16...  3.07 us

profile of v2, /device:TPU:39, one launch (start us, length us, event | category | flops | bytes accessed | tf_op | source)
XLA Modules:
  0.0 70.9 jit_solution(5207637678464451881)
XLA Ops:
  1.3 66.4 %shard_map.93 = (bf16[1,192,1536]{2,1,0:T(8,128)(2,1)}, bf16[1,192,2304]{2,1,0:T(8,128)(2,1)}, f32[8,896]{1,0:T(8,128)}) custom-call(bf16[1,192,1536]{2,1,0:T(8,128)(2,1)} %resid_h.1, bf16[1,192,2304]{2,1,0:T(8,128)(2,1)} %qkv_h.1, bf16[1,192,1536]{2,1,0:T(8,128)(2,1)} %cot_h.1, s32[1]{0:T(128)S(6)} %copy.10.len_s, bf16[768,1536]{1,0:T(8,128)(2,1)} %proj_h.1, ...), custom_call_target="tpu_custom_call" | custom-call | flops 3000000000 | bytes 8000000 | tf_op jit(solution)/shard_map/pallas_call | solution.py:496
  67.7 3.1 %shard_map.94 = (bf16[1,192,1536]{2,1,0:T(8,128)(2,1)}, bf16[1,192,2304]{2,1,0:T(8,128)(2,1)}, f32[6,768]{1,0:T(8,128)}, f32[6,31]{1,0:T(8,128)}) custom-call(bf16[1,192,1536]{2,1,0:T(8,128)(2,1)} %get-tuple-element.11.dres_i, bf16[1,192,2304]{2,1,0:T(8,128)(2,1)} %get-tuple-element.12.dqkv_i, f32[8,896]{1,0:T(8,128)} %get-tuple-element.13.sums_i), custom_call_target="tpu_custom_call" | custom-call | bytes 4000000 | tf_op jit(solution)/shard_map/pallas_call | solution.py:520

commit v3 on v2

--- a/solution.py
+++ b/solution.py
@@ -50,9 +50,9 @@
 
 def kernel(
     resid_h, qkv_h, cot_h, len_s, proj_h, ker_h,
-    dres_h, dqkv_h, sums_o,
+    dres_v, out_v, sums_o,
     q_all, kv, res_v, cot_v, w_v, ker_v, probs, probs_k, stat, att_v, att_m, go,
-    mext, gext, dres_v, out_v, hs, hm, hc, kt, kt_part, kt_all, turned, lhs_own, lhs_out, lhs_in,
+    mext, gext, hs, hm, hc, kt_part, lhs_own, lhs_out, lhs_in,
     s_2hop, r_2hop, s_up, s_down, keep_up, keep_down, r_up, r_down, own_1,
     s_2, r_2, own_2, s_3, r_3,
     loc_sem, nb_send, nb_recv, rs_send, rs_recv,
@@ -144,8 +144,12 @@
     has_right = (tm < 63).astype(F32)
     lane = lax.broadcasted_iota(jnp.int32, (1, 128), 1)
 
-    kt[...] = jnp.zeros_like(kt)
-    att_v[T:256, :] = jnp.zeros((256 - T, W), BF16)
+    eye_row = lax.broadcasted_iota(jnp.int32, (256 - T, 128), 0)
+    eye_col = lax.broadcasted_iota(jnp.int32, (256 - T, 128), 1)
+    att_v[T:256, 0:W] = jnp.zeros((256 - T, W), BF16)
+    att_v[0:T, W:RW] = jnp.zeros((T, 128), BF16)
+    att_v[T:256, W:RW] = ((eye_row == eye_col) & (eye_row < 32)).astype(F32).astype(BF16)
+    dres_v[T:256, :] = jnp.zeros((256 - T, D), BF16)
     s_3[...] = jnp.zeros_like(s_3)
 
     wait(ins)
@@ -186,7 +190,7 @@
 
     def project(j, carry):
         cols = lanes(j, 256)
-        mixed = res_v[:, cols].astype(F32) + dot(att_v[0:T, :], w_v[:, cols], 1, 0)
+        mixed = res_v[:, cols].astype(F32) + dot(att_v[0:T, 0:W], w_v[:, cols], 1, 0)
         masked = (mixed.astype(BF16).astype(F32) * valid).astype(BF16)
         hs[0, :, cols] = masked[0:REACH]
         hs[1, :, cols] = masked[T - REACH : T]
@@ -240,6 +244,8 @@
             kernel_terms(c, row, 80, sums)
         for j in range(TAPS):
             kt_part[c, 8 * j : 8 * j + 8, :] = sums[j]
+        back_rows(c, 32, 64)
+        back_rows(c, 96, 64)
         return carry
 
     lax.fori_loop(0, CHUNKS // 2, conv_inner, 0)
@@ -253,7 +259,7 @@
     wait(early)
     wait(mask_halo)
 
-    def edges_and_back(c, carry):
+    def edges_and_back(c):
         cols = lanes(c, 128)
         mext[c, 0:REACH, :] = hm[0, :, cols].astype(F32) * has_left
         mext[c, REACH + T : 2 * REACH + T, :] = hm[1, :, cols].astype(F32) * has_right
@@ -267,39 +273,53 @@
         kernel_terms(c, 0, EDGE, sums)
         kernel_terms(c, T - EDGE, EDGE, sums)
         for j in range(TAPS):
-            kt[j : j + 1, :] = jnp.sum(sums[j], axis=0, keepdims=True)
-        kt_all[cols, :] = kt[...].T
-        back_rows(c, 0, 96)
-        back_rows(c, 96, 96)
-        grad = dres_v[:, cols].astype(F32)
-        turned[cols, :] = jnp.concatenate([grad, jnp.zeros((256 - T, 128), F32)], axis=0).T
+            kt_part[c, 8 * j : 8 * j + 8, :] = sums[j]
+        back_rows(c, 0, 32)
+        back_rows(c, T - 32, 32)
+
+    tap_row = lax.broadcasted_iota(jnp.int32, (32, 8 * TAPS), 0)
+    tap_col = lax.broadcasted_iota(jnp.int32, (32, 8 * TAPS), 1)
+    adder = (tap_col // 8 == tap_row).astype(F32).astype(BF16)
+
+    def pair_copy(q):
+        quarter = pl.ds(4 * q, 4)
+        return far(lhs_out.at[quarter], lhs_in.at[quarter], 15 + q, mate)
+
+    def finish(q):
+        cols = lanes(q, 384)
+        terms = jnp.concatenate([kt_part[3 * q + i].astype(BF16) for i in range(3)], axis=1)
+        dres_v[T : T + 32, cols] = dot(adder, terms, 1, 0).astype(BF16)
+        turned = dres_v[:, cols].T.astype(F32)
+        for part in range(4):
+            row = 96 * part
+            both = [
+                jnp.concatenate(
+                    [turned[row + 24 * i : row + 24 * i + 24], turned[row + 48 + 24 * i : row + 72 + 24 * i]],
+                    axis=0,
+                )
+                for i in range(2)
+            ]
+            lhs_own[4 * q + part] = jnp.where(core == 0, both[0], both[1]).astype(BF16)
+            lhs_out[4 * q + part] = jnp.where(core == 0, both[1], both[0]).astype(BF16)
+        pair_copy(q).start()
+
+    def one_chunk(c, carry):
+        edges_and_back(c)
         return carry
 
-    def rows_of(ref, block, which):
-        row = block * 96 + which * 24
-        return jnp.concatenate(
-            [
-                ref[pl.ds(pl.multiple_of(row, 8), 24), :],
-                ref[pl.ds(pl.multiple_of(row + 48, 8), 24), :],
-            ],
-            axis=0,
-        )
-
-    pair_copies = []
-    for quarter in range(4):
-        lax.fori_loop(3 * quarter, 3 * quarter + 3, edges_and_back, 0)
-        for block in range(4 * quarter, 4 * quarter + 4):
-            lhs_out[block, :, 0:256] = rows_of(turned, block, other).astype(BF16)
-            lhs_out[block, :, 256:384] = rows_of(kt_all, block, other).astype(BF16)
-        quarters = slice(4 * quarter, 4 * quarter + 4)
-        pair_copies += start([far(lhs_out.at[quarters], lhs_in.at[quarters], 15 + quarter, mate)])
-    out_resid = start([local(dres_v, dres_h.at[0], 6)])
+    def quarter(q, carry):
+        lax.fori_loop(3 * q, 3 * q + 3, one_chunk, 0)
+        finish(q)
+        return carry
+
+    lax.fori_loop(0, 4, quarter, 0)
+    pair_copies = [pair_copy(q) for q in range(4)]
 
     place, second = y * other + x * core, x * other + y * core
 
     def attended_grad(j, carry):
         go[own, pl.ds(pl.multiple_of(128 + j * 256, 128), 256)] = (
-            valid * dot(dres_v[...], w_v[lanes(j, 256), :], 1, 1)
+            valid * dot(dres_v[0:T, :], w_v[lanes(j, 256), :], 1, 1)
         ).astype(BF16)
         return carry
 
@@ -327,26 +347,13 @@
 
     grad_copies = [send_grads(first, 18)]
 
-    def gather_own(block, carry):
-        lhs_own[block] = rows_of(turned, block, core).astype(BF16)
-        return carry
-
-    lax.fori_loop(0, 16, gather_own, 0)
     wait(pair_copies)
 
     def pair_sum(a):
         blocks = [(a * other + b * core) * 4 + b * other + a * core for b in range(4)]
         mine = jnp.concatenate([lhs_own[block] for block in blocks], axis=0)
-        theirs = jnp.concatenate([lhs_in[block, :, 0:256] for block in blocks], axis=0)
-        main = dot(mine, att_v[...], 1, 0) + dot(theirs, att_m[...], 1, 0)
-        side = jnp.concatenate(
-            [
-                rows_of(kt_all, block, core) + lhs_in[block, :, 256:384].astype(F32)
-                for block in blocks
-            ],
-            axis=0,
-        )
-        return jnp.concatenate([main, side], axis=1)
+        theirs = jnp.concatenate([lhs_in[block] for block in blocks], axis=0)
+        return dot(mine, att_v[...], 1, 0) + dot(theirs, att_m[...], 1, 0)
 
     half = 96
     whole = pair_sum((place + 2) % 4)
@@ -451,21 +458,18 @@
 
     wait(grad_copies[1])
     key_group(1)
-    out_qkv = start([local(out_v, dqkv_h.at[0], 7)])
 
     wait(z_copies)
     total = s_3[zl * 4 + zh]
     for e in range(7):
         total = total + r_3[e]
     sums_o[...] = total
-    wait(out_resid)
-    wait(out_qkv)
 
 
 def hand_over(dres_i, dqkv_i, sums_i, dres_o, dqkv_o, dproj_o, dker_o, sem):
     copies = [
-        pltpu.make_async_copy(dres_i, dres_o, sem.at[0]),
-        pltpu.make_async_copy(dqkv_i, dqkv_o, sem.at[1]),
+        pltpu.make_async_copy(dres_i.at[0:T], dres_o.at[0], sem.at[0]),
+        pltpu.make_async_copy(dqkv_i, dqkv_o.at[0], sem.at[1]),
     ]
     for copy in copies:
         copy.start()
@@ -481,12 +485,11 @@
     scratch = [
         ((KEYS, W), BF16), ((KEYS, 2 * W), BF16), ((T, D), BF16), ((T, D), BF16),
         ((W, D), BF16), ((TAPS, D), F32), ((H, T, KEYS), BF16), ((H, KEYS, T), BF16),
-        ((KEYS, 128), F32), ((256, W), BF16), ((256, W), BF16), ((KEYS, RW), BF16),
-        ((CHUNKS, T + 2 * REACH, 128), F32), ((CHUNKS, T + 2 * EDGE, 128), F32), ((T, D), BF16),
-        ((T, 3 * W), BF16),
+        ((KEYS, 128), F32), ((256, RW), BF16), ((256, RW), BF16), ((KEYS, RW), BF16),
+        ((CHUNKS, T + 2 * REACH, 128), F32), ((CHUNKS, T + 2 * EDGE, 128), F32),
         ((2, REACH, D), BF16), ((2, REACH, D), BF16), ((2, EDGE, D), BF16),
-        ((128, 128), F32), ((CHUNKS, 8 * TAPS, 128), F32), ((D, 128), F32), ((D, 256), F32),
-        ((16, 48, 256), BF16), ((16, 48, 384), BF16), ((16, 48, 384), BF16),
+        ((CHUNKS, 8 * TAPS, 128), F32),
+        ((16, 48, 256), BF16), ((16, 48, 256), BF16), ((16, 48, 256), BF16),
         ((T, RW), BF16), ((T, RW), BF16), ((T, RW), BF16), ((T, RW), BF16),
         ((T // 2, RW), F32), ((T // 2, RW), F32), ((T, RW), BF16), ((T, RW), BF16),
         ((T, RW), F32),
@@ -496,12 +499,12 @@
     dres, dqkv, sums = pl.pallas_call(
         kernel,
         out_shape=[
-            jax.ShapeDtypeStruct((1, T, D), BF16),
-            jax.ShapeDtypeStruct((1, T, 3 * W), BF16),
-            jax.ShapeDtypeStruct((8, RW), F32),
+            pltpu.VMEM((256, D), BF16),
+            pltpu.VMEM((T, 3 * W), BF16),
+            pltpu.VMEM((8, RW), F32),
         ],
         in_specs=[hbm, hbm, hbm, pl.BlockSpec(memory_space=pltpu.SMEM), hbm, hbm],
-        out_specs=[hbm, hbm, vmem],
+        out_specs=[vmem, vmem, vmem],
         scratch_shapes=[pltpu.VMEM(shape, kind) for shape, kind in scratch]
         + [
             pltpu.SemaphoreType.DMA((8,)),
@@ -511,7 +514,7 @@
             pltpu.SemaphoreType.DMA((26,)),
         ],
         compiler_params=pltpu.CompilerParams(
-            collective_id=0, has_side_effects=True, vmem_limit_bytes=56 * 2**20
+            collective_id=0, has_side_effects=True, vmem_limit_bytes=60 * 2**20
         ),
         cost_estimate=pl.CostEstimate(
             flops=3_000_000_000, bytes_accessed=8_000_000, transcendentals=1_000_000
@@ -528,6 +531,7 @@
         in_specs=[vmem, vmem, vmem],
         out_specs=[hbm, hbm, vmem, vmem],
         scratch_shapes=[pltpu.SemaphoreType.DMA((2,))],
+        compiler_params=pltpu.CompilerParams(vmem_limit_bytes=8 * 2**20),
         cost_estimate=pl.CostEstimate(flops=0, bytes_accessed=4_000_000, transcendentals=0),
     )(dres, dqkv, sums)
     return dres, dqkv, dproj.T, dker.T

time: 71 us -> 66.2 us (0.932)
  the two profiles are of different devices: /device:TPU:39 before, /device:TPU:1 now
where the time goes in v3:
time: 66.2 us; the launch traced here: 65.4 us
  Pallas kernels  64 us (97%)
  between operations  1.45 us (2%)
    pallas_call x1, Pallas kernels, local(): pl.pallas_call(kernel, out_shape=[pltpu.VMEM((256, D), BF16), pltpu.VMEM(...  62.3 us
    pallas_call x1, Pallas kernels, local(): pl.pallas_call(hand_over, out_shape=[jax.ShapeDtypeStruct((1, T, D), BF16...  1.73 us

profile of v3, /device:TPU:1, one launch (start us, length us, event | category | flops | bytes accessed | tf_op | source)
XLA Modules:
  0.0 65.4 jit_solution(6381843223530663660)
XLA Ops:
  1.3 62.3 %shard_map.93 = (bf16[256,1536]{1,0:T(8,128)(2,1)S(1)}, bf16[192,2304]{1,0:T(8,128)(2,1)S(1)}, f32[8,896]{1,0:T(8,128)S(1)}) custom-call(bf16[1,192,1536]{2,1,0:T(8,128)(2,1)} %resid_h.1, bf16[1,192,2304]{2,1,0:T(8,128)(2,1)} %qkv_h.1, bf16[1,192,1536]{2,1,0:T(8,128)(2,1)} %cot_h.1, s32[1]{0:T(128)S(6)} %copy.10.len_s, bf16[768,1536]{1,0:T(8,128)(2,1)} %proj_h.1, ...), custom_call_target="tpu_custom_call" | custom-call | flops 3000000000 | bytes 8000000 | tf_op jit(solution)/shard_map/pallas_call | solution.py:499
  63.5 1.7 %shard_map.94 = (bf16[1,192,1536]{2,1,0:T(8,128)(2,1)}, bf16[1,192,2304]{2,1,0:T(8,128)(2,1)}, f32[6,768]{1,0:T(8,128)}, f32[6,31]{1,0:T(8,128)}) custom-call(bf16[256,1536]{1,0:T(8,128)(2,1)S(1)} %get-tuple-element.11.dres_i, bf16[192,2304]{1,0:T(8,128)(2,1)S(1)} %get-tuple-element.12.dqkv_i, f32[8,896]{1,0:T(8,128)S(1)} %get-tuple-element.13.sums_i), custom_call_target="tpu_custom_call" | custom-call | bytes 4000000 | tf_op jit(solution)/shard_map/pallas_call | solution.py:523

commit v4 on v3

--- a/solution.py
+++ b/solution.py
@@ -52,7 +52,7 @@
     resid_h, qkv_h, cot_h, len_s, proj_h, ker_h,
     dres_v, out_v, sums_o,
     q_all, kv, res_v, cot_v, w_v, ker_v, probs, probs_k, stat, att_v, att_m, go,
-    mext, gext, hs, hm, hc, kt_part, lhs_own, lhs_out, lhs_in,
+    mext, gext, hs, hm, hc, mix, kt_part, lhs_own, lhs_out, lhs_in,
     s_2hop, r_2hop, s_up, s_down, keep_up, keep_down, r_up, r_down, own_1,
     s_2, r_2, own_2, s_3, r_3,
     loc_sem, nb_send, nb_recv, rs_send, rs_recv,
@@ -119,6 +119,7 @@
     everyone = [left, right, up, down] + second_peers + [peer for peer, _ in z_peers]
     for peer in everyone:
         pl.semaphore_signal(barrier, inc=1, device_id=peer, device_id_type=MESH)
+
     pl.semaphore_wait(barrier, len(everyone))
 
     kv_copies = []
@@ -175,7 +176,15 @@
         att_v[0:T, base : base + GROUP] = (join_heads(outs) * valid).astype(BF16)
         return stats
 
+    def project_half(j, carry):
+        cols = lanes(j, 256)
+        mix[:, cols] = res_v[:, cols].astype(F32) + dot(
+            att_v[0:T, 0:GROUP], w_v[0:GROUP, cols], 1, 0
+        )
+        return carry
+
     stats = forward_group(0, jnp.zeros((T, 128), F32))
+    lax.fori_loop(0, D // 256, project_half, 0)
     wait(kv_copies[4:])
     early = start([
         near(cot_v.at[0:EDGE], hc.at[1], 8, left),
@@ -190,7 +199,7 @@
 
     def project(j, carry):
         cols = lanes(j, 256)
-        mixed = res_v[:, cols].astype(F32) + dot(att_v[0:T, 0:W], w_v[:, cols], 1, 0)
+        mixed = mix[:, cols] + dot(att_v[0:T, GROUP:W], w_v[GROUP:W, cols], 1, 0)
         masked = (mixed.astype(BF16).astype(F32) * valid).astype(BF16)
         hs[0, :, cols] = masked[0:REACH]
         hs[1, :, cols] = masked[T - REACH : T]
@@ -324,6 +333,22 @@
         return carry
 
     lax.fori_loop(0, W // 256, attended_grad, 0)
+    wait(pair_copies)
+
+    def pair_sum(a):
+        blocks = [(a * other + b * core) * 4 + b * other + a * core for b in range(4)]
+        mine = jnp.concatenate([lhs_own[block] for block in blocks], axis=0)
+        theirs = jnp.concatenate([lhs_in[block] for block in blocks], axis=0)
+        return dot(mine, att_v[...], 1, 0) + dot(theirs, att_m[...], 1, 0)
+
+    half = 96
+    whole = pair_sum((place + 2) % 4)
+    s_2hop[0:half] = whole[0:half].astype(BF16)
+    s_2hop[half:T] = whole[half:T].astype(BF16)
+    two_hop = start([
+        far(s_2hop.at[0:half], r_2hop.at[0:half], 1, up),
+        far(s_2hop.at[half:T], r_2hop.at[half:T], 2, down),
+    ])
     deltas = jnp.zeros((T, 128), F32)
     for head in range(H):
         start_, width = WINDOWS[head % 4]
@@ -347,22 +372,6 @@
 
     grad_copies = [send_grads(first, 18)]
 
-    wait(pair_copies)
-
-    def pair_sum(a):
-        blocks = [(a * other + b * core) * 4 + b * other + a * core for b in range(4)]
-        mine = jnp.concatenate([lhs_own[block] for block in blocks], axis=0)
-        theirs = jnp.concatenate([lhs_in[block] for block in blocks], axis=0)
-        return dot(mine, att_v[...], 1, 0) + dot(theirs, att_m[...], 1, 0)
-
-    half = 96
-    whole = pair_sum((place + 2) % 4)
-    s_2hop[0:half] = whole[0:half].astype(BF16)
-    s_2hop[half:T] = whole[half:T].astype(BF16)
-    two_hop = start([
-        far(s_2hop.at[0:half], r_2hop.at[0:half], 1, up),
-        far(s_2hop.at[half:T], r_2hop.at[half:T], 2, down),
-    ])
     whole = pair_sum((place + 1) % 4)
     keep_up[...] = whole[0:half]
     s_up[half:T] = whole[half:T].astype(BF16)
@@ -434,7 +443,7 @@
     wait(one_hop)
     grad_copies.append(send_grads(last, 20))
     second_copies = []
-    for s in range(4):
+    for s in (1, 0, 2, 3):
         rows = pl.ds(pl.multiple_of((second + 1 + s) % 4 * 48, 16), 48)
         total = own_1[rows, :] + r_up[rows, :].astype(F32) + r_down[rows, :].astype(F32)
         if s < 3:
@@ -453,7 +462,8 @@
     for part in range(8):
         s_3[part, 0:6, :] = total[part * 6 : part * 6 + 6]
     z_copies = []
-    for e, (peer, part) in enumerate(z_peers):
+    for e in (3, 2, 4, 1, 5, 0, 6):
+        peer, part = z_peers[e]
         z_copies += start([far(s_3.at[part], r_3.at[e], 19 + e, peer)])
 
     wait(grad_copies[1])
@@ -466,15 +476,19 @@
     sums_o[...] = total
 
 
-def hand_over(dres_i, dqkv_i, sums_i, dres_o, dqkv_o, dproj_o, dker_o, sem):
+def hand_over(dres_i, dqkv_i, sums_i, dres_o, dqkv_o, dproj_o, dker_o, proj_v, ker_v, sem):
     copies = [
-        pltpu.make_async_copy(dres_i.at[0:T], dres_o.at[0], sem.at[0]),
-        pltpu.make_async_copy(dqkv_i, dqkv_o.at[0], sem.at[1]),
+        pltpu.make_async_copy(dqkv_i, dqkv_o.at[0], sem.at[0]),
+        pltpu.make_async_copy(dres_i.at[0:T], dres_o.at[0], sem.at[1]),
+        pltpu.make_async_copy(proj_v, dproj_o, sem.at[2]),
+        pltpu.make_async_copy(ker_v, dker_o, sem.at[3]),
     ]
-    for copy in copies:
-        copy.start()
-    dproj_o[...] = sums_i[0:6, 0:W]
-    dker_o[...] = sums_i[0:6, W : W + TAPS]
+    copies[0].start()
+    copies[1].start()
+    proj_v[...] = sums_i[0:6, 0:W]
+    copies[2].start()
+    ker_v[...] = sums_i[0:6, W : W + TAPS]
+    copies[3].start()
     for copy in copies:
         copy.wait()
 
@@ -487,7 +501,7 @@
         ((W, D), BF16), ((TAPS, D), F32), ((H, T, KEYS), BF16), ((H, KEYS, T), BF16),
         ((KEYS, 128), F32), ((256, RW), BF16), ((256, RW), BF16), ((KEYS, RW), BF16),
         ((CHUNKS, T + 2 * REACH, 128), F32), ((CHUNKS, T + 2 * EDGE, 128), F32),
-        ((2, REACH, D), BF16), ((2, REACH, D), BF16), ((2, EDGE, D), BF16),
+        ((2, REACH, D), BF16), ((2, REACH, D), BF16), ((2, EDGE, D), BF16), ((T, D), F32),
         ((CHUNKS, 8 * TAPS, 128), F32),
         ((16, 48, 256), BF16), ((16, 48, 256), BF16), ((16, 48, 256), BF16),
         ((T, RW), BF16), ((T, RW), BF16), ((T, RW), BF16), ((T, RW), BF16),
@@ -529,8 +543,12 @@
             jax.ShapeDtypeStruct((6, TAPS), F32),
         ],
         in_specs=[vmem, vmem, vmem],
-        out_specs=[hbm, hbm, vmem, vmem],
-        scratch_shapes=[pltpu.SemaphoreType.DMA((2,))],
+        out_specs=[hbm, hbm, hbm, hbm],
+        scratch_shapes=[
+            pltpu.VMEM((6, W), F32),
+            pltpu.VMEM((6, TAPS), F32),
+            pltpu.SemaphoreType.DMA((4,)),
+        ],
         compiler_params=pltpu.CompilerParams(vmem_limit_bytes=8 * 2**20),
         cost_estimate=pl.CostEstimate(flops=0, bytes_accessed=4_000_000, transcendentals=0),
     )(dres, dqkv, sums)

time: 66.2 us -> 62.9 us (0.950)
  Pallas kernels: 64 us -> 61.2 us
    pallas_call x1, Pallas kernels: 62.3 us -> 60.1 us  [local(): pl.pallas_call(kernel, out_shape=[pltpu.VMEM((256, D), BF16), pltpu.VMEM(...]
where the time goes in v4:
time: 62.9 us; the launch traced here: 62.5 us
  Pallas kernels  61.2 us (97%)
  between operations  1.29 us (2%)
    pallas_call x1, Pallas kernels, local(): pl.pallas_call(kernel, out_shape=[pltpu.VMEM((256, D), BF16), pltpu.VMEM(...  60.1 us

profile of v4, /device:TPU:1, one launch (start us, length us, event | category | flops | bytes accessed | tf_op | source)
XLA Modules:
  0.0 62.5 jit_solution(2069749585649560250)
XLA Ops:
  1.3 60.1 %shard_map.93 = (bf16[256,1536]{1,0:T(8,128)(2,1)S(1)}, bf16[192,2304]{1,0:T(8,128)(2,1)S(1)}, f32[8,896]{1,0:T(8,128)S(1)}) custom-call(bf16[1,192,1536]{2,1,0:T(8,128)(2,1)} %resid_h.1, bf16[1,192,2304]{2,1,0:T(8,128)(2,1)} %qkv_h.1, bf16[1,192,1536]{2,1,0:T(8,128)(2,1)} %cot_h.1, s32[1]{0:T(128)S(6)} %copy.10.len_s, bf16[768,1536]{1,0:T(8,128)(2,1)} %proj_h.1, ...), custom_call_target="tpu_custom_call" | custom-call | flops 3000000000 | bytes 8000000 | tf_op jit(solution)/shard_map/pallas_call | solution.py:513
  61.4 1.1 %shard_map.94 = (bf16[1,192,1536]{2,1,0:T(8,128)(2,1)}, bf16[1,192,2304]{2,1,0:T(8,128)(2,1)}, f32[6,768]{1,0:T(8,128)}, f32[6,31]{1,0:T(8,128)}) custom-call(bf16[256,1536]{1,0:T(8,128)(2,1)S(1)} %get-tuple-element.11.dres_i, bf16[192,2304]{1,0:T(8,128)(2,1)S(1)} %get-tuple-element.12.dqkv_i, f32[8,896]{1,0:T(8,128)S(1)} %get-tuple-element.13.sums_i), custom_call_target="tpu_custom_call" | custom-call | bytes 4000000 | tf_op jit(solution)/shard_map/pallas_call | solution.py:537

commit v5 on v4

--- a/solution.py
+++ b/solution.py
@@ -441,7 +441,6 @@
     probs_group(1)
 
     wait(one_hop)
-    grad_copies.append(send_grads(last, 20))
     second_copies = []
     for s in (1, 0, 2, 3):
         rows = pl.ds(pl.multiple_of((second + 1 + s) % 4 * 48, 16), 48)
@@ -451,6 +450,7 @@
             second_copies += start([far(s_2.at[s], r_2.at[s], 7 + s, second_peers[s])])
         else:
             own_2[...] = total
+    grad_copies.append(send_grads(last, 20))
 
     wait(grad_copies[0])
     key_group(0)

time: 62.9 us -> 62.9 us (level)
  no operation moved by 1% of the time
where the time goes in v5:
time: 62.9 us; the launch traced here: 62.5 us
  Pallas kernels  61.2 us (97%)
  between operations  1.29 us (2%)
    pallas_call x1, Pallas kernels, local(): pl.pallas_call(kernel, out_shape=[pltpu.VMEM((256, D), BF16), pltpu.VMEM(...  60.1 us

profile of v5, /device:TPU:1, one launch (start us, length us, event | category | flops | bytes accessed | tf_op | source)
XLA Modules:
  0.0 62.5 jit_solution(15814421839194290209)
XLA Ops:
  1.3 60.1 %shard_map.93 = (bf16[256,1536]{1,0:T(8,128)(2,1)S(1)}, bf16[192,2304]{1,0:T(8,128)(2,1)S(1)}, f32[8,896]{1,0:T(8,128)S(1)}) custom-call(bf16[1,192,1536]{2,1,0:T(8,128)(2,1)} %resid_h.1, bf16[1,192,2304]{2,1,0:T(8,128)(2,1)} %qkv_h.1, bf16[1,192,1536]{2,1,0:T(8,128)(2,1)} %cot_h.1, s32[1]{0:T(128)S(6)} %copy.10.len_s, bf16[768,1536]{1,0:T(8,128)(2,1)} %proj_h.1, ...), custom_call_target="tpu_custom_call" | custom-call | flops 3000000000 | bytes 8000000 | tf_op jit(solution)/shard_map/pallas_call | solution.py:513
  61.4 1.1 %shard_map.94 = (bf16[1,192,1536]{2,1,0:T(8,128)(2,1)}, bf16[1,192,2304]{2,1,0:T(8,128)(2,1)}, f32[6,768]{1,0:T(8,128)}, f32[6,31]{1,0:T(8,128)}) custom-call(bf16[256,1536]{1,0:T(8,128)(2,1)S(1)} %get-tuple-element.11.dres_i, bf16[192,2304]{1,0:T(8,128)(2,1)S(1)} %get-tuple-element.12.dqkv_i, f32[8,896]{1,0:T(8,128)S(1)} %get-tuple-element.13.sums_i), custom_call_target="tpu_custom_call" | custom-call | bytes 4000000 | tf_op jit(solution)/shard_map/pallas_call | solution.py:537
